TPU v7x, 256 devices: a whole 4x4x8 slice. The times are simulated.
256 devices in a mesh: rep: 32 (over y_hi, z, core), seq: 8 (over y_lo, x).
Axes of the slice: x: 4, y: 4 (y_hi: 2, y_lo: 2; y = y_hi * 2 + y_lo), z: 8, core: 2. Of those that a mesh axis runs over, the one named last changes fastest.
Arguments:
- text_tokens: bfloat16 [32, 512, 3072], P('rep', 'seq'), may hold values from -6 to 6
- image_tokens: bfloat16 [32, 576, 3072], P('rep', 'seq'), may hold values from -6 to 6
- weights: bfloat16 [2, 3072, 3, 3072], P(None, ('rep', 'seq'))
- qk_gain: float32 [2, 2, 128], replicated, may hold values from 0.5 to 4.2, as said below
- mod_table: float32 [28, 2, 2, 3072], replicated, may hold values from -3 to 3
- text_lengths: int32 [32], P('rep'), may hold values from 64 to 512, as said below
- time_index: int32 [32], P('rep'), may hold values from 0 to 27
Outputs:
- attended_text: bfloat16 [32, 512, 3072], P('rep', 'seq')
- attended_image: bfloat16 [32, 576, 3072], P('rep', 'seq')
Inputs may be any that keep to these rules, and one draw needn't show every extreme that they name: `text_lengths`: padding of a prompt lies past its length; some prompt fills all 512 text tokens. `qk_gain`: positive gains.
All inputs are finite; a program needn't handle non-finite values.
Results may differ from a plain program's by a relative error of at most 0.01.
Values may be sent and summed in bfloat16 or wider, within the bound.
A program may use at most 128 MiB of HBM per device.

v0:
```python
import jax
import jax.numpy as jnp
from jax import lax
from jax.sharding import PartitionSpec as P

D = 3072
HD = 128
GRID = 24
TXT = 512


def layer_modulate(tokens, shift_row, scale_row):
    values = tokens.astype(jnp.float32)
    center = values - jnp.mean(values, axis=-1, keepdims=True)
    spread = jnp.mean(center * center, axis=-1, keepdims=True)
    normed = center * lax.rsqrt(spread + 1e-06)
    return (normed * (1.0 + shift_row * 0.0 + scale_row) + shift_row).astype(jnp.bfloat16)


def rope_tables(length, text_count, grid_side, head_dim):
    pair_count = head_dim // 2
    still_pairs = head_dim // 16
    row_pairs = (pair_count - still_pairs) // 2
    col_pairs = pair_count - still_pairs - row_pairs
    position = jnp.arange(length, dtype=jnp.int32)
    image_pos = jnp.maximum(position - text_count, 0)
    is_image = (position >= text_count).astype(jnp.float32)
    row_pos = (image_pos // grid_side).astype(jnp.float32) * is_image
    col_pos = (image_pos % grid_side).astype(jnp.float32) * is_image
    row_freq = 10000.0 ** (-jnp.arange(row_pairs, dtype=jnp.float32) / row_pairs)
    col_freq = 10000.0 ** (-jnp.arange(col_pairs, dtype=jnp.float32) / col_pairs)
    angles = jnp.concatenate(
        [
            jnp.zeros((length, still_pairs), jnp.float32),
            row_pos[:, None] * row_freq[None, :],
            col_pos[:, None] * col_freq[None, :],
        ],
        axis=1,
    )
    return (jnp.cos(angles), jnp.sin(angles))


def rotate(values, cosine, sine):
    shaped = values.reshape(values.shape[0], values.shape[1], -1, 2)
    first_part = shaped[..., 0]
    second_part = shaped[..., 1]
    cos_part = cosine[:, None, :]
    sin_part = sine[:, None, :]
    turned = jnp.stack(
        [
            first_part * cos_part - second_part * sin_part,
            first_part * sin_part + second_part * cos_part,
        ],
        axis=-1,
    )
    return turned.reshape(values.shape)


def normalize_heads(values, gain):
    power = jnp.mean(values * values, axis=-1, keepdims=True)
    return values * lax.rsqrt(power + 1e-06) * gain


def prepare_heads(projected, gain, cosine, sine):
    query = rotate(normalize_heads(projected[:, 0], gain[0]), cosine, sine).astype(jnp.bfloat16)
    key_part = rotate(normalize_heads(projected[:, 1], gain[1]), cosine, sine).astype(jnp.bfloat16)
    value_part = projected[:, 2].astype(jnp.bfloat16)
    return (query, key_part, value_part)


def attend_head(query_head, key_head, value_head, allowed):
    scores = lax.dot_general(
        query_head, key_head, (((1,), (1,)), ((), ())), preferred_element_type=jnp.float32
    )
    scores = scores * query_head.shape[-1] ** (-0.5)
    scores = jnp.where(allowed[None, :], scores, -jnp.inf)
    row_max = jnp.max(scores, axis=-1, keepdims=True)
    exponent = jnp.exp(scores - row_max)
    softmax_out = (exponent / jnp.sum(exponent, axis=-1, keepdims=True)).astype(jnp.bfloat16)
    return jnp.dot(softmax_out, value_head, preferred_element_type=jnp.float32).astype(jnp.bfloat16)


def run_attention(queries, keys_all, values_all, allowed):

    def one_head(trio):
        return attend_head(trio[0], trio[1], trio[2], allowed)

    stacked = (
        jnp.moveaxis(queries, 1, 0),
        jnp.moveaxis(keys_all, 1, 0),
        jnp.moveaxis(values_all, 1, 0),
    )
    outputs = lax.map(one_head, stacked)
    outputs = jnp.moveaxis(outputs, 0, 1)
    return outputs.reshape(outputs.shape[0], -1)


def on_device(text_tokens, image_tokens, weights, qk_gain, mod_table, text_lengths, time_index):
    seq_count = lax.axis_size("seq")
    col_count = weights.shape[3] // seq_count
    heads_here = col_count // HD
    total_rows = TXT + GRID * GRID
    cosine_all, sine_all = rope_tables(total_rows, TXT, GRID, HD)
    picker = (jnp.arange(mod_table.shape[0], dtype=jnp.int32) == time_index[0]).astype(jnp.float32)
    table_row = jnp.sum(mod_table * picker[:, None, None, None], axis=0)
    prepared = []
    for stream in range(2):
        rows_here = (text_tokens, image_tokens)[stream][0]
        modded = layer_modulate(rows_here, table_row[stream, 0], table_row[stream, 1])
        relaid = lax.all_to_all(weights[stream], "seq", split_axis=2, concat_axis=0, tiled=True)
        full_weight = lax.all_gather(relaid, "rep", axis=0, tiled=True)
        all_rows = lax.all_gather(modded, "seq", axis=0, tiled=True)
        projected = jnp.dot(
            all_rows, full_weight.reshape(D, 3 * col_count), preferred_element_type=jnp.float32
        )
        row_count = projected.shape[0]
        offset_rows = 0 if stream == 0 else TXT
        projected = projected.reshape(row_count, 3, heads_here, HD)
        prepared.append(
            prepare_heads(
                projected,
                qk_gain[stream],
                cosine_all[offset_rows : offset_rows + row_count],
                sine_all[offset_rows : offset_rows + row_count],
            )
        )
    queries = jnp.concatenate([prepared[0][0], prepared[1][0]], axis=0)
    keys_all = jnp.concatenate([prepared[0][1], prepared[1][1]], axis=0)
    values_all = jnp.concatenate([prepared[0][2], prepared[1][2]], axis=0)
    position = jnp.arange(total_rows, dtype=jnp.int32)
    allowed = (position >= TXT) | (position < text_lengths[0])
    joined = run_attention(queries, keys_all, values_all, allowed)
    text_out, image_out = (
        lax.all_to_all(joined[:TXT], "seq", split_axis=0, concat_axis=1, tiled=True),
        lax.all_to_all(joined[TXT:], "seq", split_axis=0, concat_axis=1, tiled=True),
    )
    return (text_out[None], image_out[None])


def solution(mesh):
    placed = (
        P("rep", "seq", None),
        P("rep", "seq", None),
        P(None, ("rep", "seq"), None, None),
        P(),
        P(),
        P("rep"),
        P("rep"),
    )
    return jax.shard_map(
        on_device,
        mesh=mesh,
        in_specs=placed,
        out_specs=(P("rep", "seq", None), P("rep", "seq", None)),
        check_vma=False,
    )
```

profile of v0, /device:TPU:1, one launch (start us, length us, event | category | flops | bytes accessed | tf_op | source)
XLA Modules:
  0.0 404.6 jit_solution(1108472939136243536)
XLA Ops:
  7.2 1.9 fusion.49
  10.0 3.3 copy.45
  13.3 3.0 reshape.216
  16.3 11.9 %all_to_all.68 = bf16[8,2,6912]{2,1,0:T(2,128)(2,1)} all-to-all(bf16[8,2,6912]{2,1,0:T(2,128)(2,1)S(1)} %reshape.216), channel_id=1, replica_groups=mesh['rep'=32,'seq'=8] {'seq'}, dimensions={0} | all-to-all | bytes 442368 | tf_op jit(solution)/shard_map/all_to_all | solution.py:110
  28.2 3.9 reshape.217
  32.1 1.8 copy.46
  34.7 4.3 %copy.41 = bf16[12,3,3072]{0,1,2:T(4,128)(2,1)S(1)} copy(bf16[12,3,3072]{2,0,1:T(8,128)(2,1)} %get-tuple-element.117) | data formatting | bytes 442368 | tf_op jit(solution)/shard_map/squeeze | solution.py:110
  39.1 3.0 reshape.218
  42.0 9.0 %all_to_all.69 = bf16[8,2,6912]{2,1,0:T(2,128)(2,1)} all-to-all(bf16[8,2,6912]{2,1,0:T(2,128)(2,1)S(1)} %reshape.218), channel_id=1, replica_groups=mesh['rep'=32,'seq'=8] {'seq'}, dimensions={0} | all-to-all | bytes 442368 | tf_op jit(solution)/shard_map/all_to_all | solution.py:110
  51.0 3.9 reshape.219
  55.0 3.0 copy.42
  58.0 1.8 all_to_all.53
  60.4 1.2 convert_reduce_fusion
  61.6 1.3 fusion.24
  62.9 2.0 multiply_reduce_fusion
  65.0 1.0 fusion.27
  67.7 1.0 fusion.38
  71.9 63.4 %all-gather.11.cloned.1.call-done = bf16[3072,3,384]{2,0,1:T(8,128)(2,1)} async-done(((bf16[96,3,384]{2,0,1:T(8,128)(2,1)}), bf16[3072,3,384]{2,0,1:T(8,128)(2,1)}) %all-gather.11.cloned.1.call-update) | async-done | bytes 7077904 | tf_op jit(solution)/shard_map/all_gather | solution.py:111
  135.3 10.3 %copy.47 = bf16[3072,3,384]{0,2,1:T(8,128)(2,1)} copy(bf16[3072,3,384]{2,0,1:T(8,128)(2,1)} %all-gather.11.cloned.1.call-done) | data formatting | bytes 14155776 | tf_op jit(solution)/shard_map/all_gather | solution.py:111
  145.6 86.1 %all-gather.7.cloned.1.call-done = bf16[3072,3,384]{2,0,1:T(8,128)(2,1)} async-done(((bf16[96,3,384]{2,0,1:T(8,128)(2,1)}), bf16[3072,3,384]{2,0,1:T(8,128)(2,1)}) %all-gather.7.cloned.1.call-update) | async-done | bytes 7077904 | tf_op jit(solution)/shard_map/all_gather | solution.py:111
  231.7 10.3 %copy.43 = bf16[3072,3,384]{0,2,1:T(8,128)(2,1)} copy(bf16[3072,3,384]{2,0,1:T(8,128)(2,1)} %all-gather.7.cloned.1.call-done) | data formatting | bytes 14155776 | tf_op jit(solution)/shard_map/all_gather | solution.py:111
  242.0 37.2 %all-gather.9.cloned.1.call-done = bf16[576,3072]{1,0:T(8,128)(2,1)} async-done(((bf16[72,3072]{1,0:T(8,128)(2,1)}), bf16[576,3072]{1,0:T(8,128)(2,1)}) %all-gather.9.cloned.1.call-update) | async-done | bytes 3538960 | tf_op jit(solution)/shard_map/all_gather | solution.py:112
  279.2 7.6 %fusion.17 = f32[576,3,3,128]{3,0,2,1:T(8,128)S(1)} fusion(bf16[3,3,128,3072]{3,2,1,0:T(8,128)(2,1)} %bitcast.144, bf16[576,3072]{1,0:T(8,128)(2,1)} %all-gather.9.cloned.1.call-done), kind=kOutput, calls=%fused_computation.21 | convolution fusion | flops 4076863488 | bytes 13271040 | tf_op jit(solution)/shard_map/dot_general | solution.py:113
  287.6 1.4 multiply_reduce_fusion.1
  288.9 36.1 %all-gather.5.cloned.1.call-done = bf16[512,3072]{1,0:T(8,128)(2,1)} async-done(((bf16[64,3072]{1,0:T(8,128)(2,1)}), bf16[512,3072]{1,0:T(8,128)(2,1)}) %all-gather.5.cloned.1.call-update) | async-done | bytes 3145744 | tf_op jit(solution)/shard_map/all_gather | solution.py:112
  325.0 7.1 %fusion.19 = f32[512,3,3,128]{0,3,2,1:T(8,128)S(1)} fusion(bf16[3,3,128,3072]{3,2,1,0:T(8,128)(2,1)} %bitcast.143, bf16[512,3072]{1,0:T(8,128)(2,1)} %all-gather.5.cloned.1.call-done), kind=kOutput, calls=%fused_computation.23 | convolution fusion | flops 3623878656 | bytes 12582912 | tf_op jit(solution)/shard_map/dot_general | solution.py:113
  332.0 1.4 multiply_reduce_fusion.3
  335.2 1.5 copy.48
  338.2 3.3 subtract_convert_fusion
  341.5 1.2 pad_maximum_fusion
  344.6 1.1 multiply_multiply_fusion.2
  346.1 3.1 subtract_convert_fusion.2
  351.2 1.2 pad_maximum_fusion.1
  352.7 2.1 pad_maximum_fusion.3
  355.7 1.1 maximum_bitcast_fusion.1
  357.9 1.0 maximum_bitcast_fusion.2
  358.9 14.8 %while.11 = (s32[]{:T(128)}, bf16[3,1088,128]{2,1,0:T(8,128)(2,1)}, bf16[3,1088,128]{2,1,0:T(8,128)(2,1)S(1)}, bf16[3,1088,128]{2,1,0:T(8,128)(2,1)S(1)}, bf16[3...) while((s32[]{:T(128)}, bf16[3,1088,128]{2,1,0:T(8,128)(2,1)}, ...), condition=%wide.region_12.13_spmd.clone, body=%wide.region_9.12_spmd.clone.sunk | while | flops 615687232 | bytes 15346073 | solution.py:93
  361.2 2.7 fusion.62
  366.1 2.7 fusion.62
  371.0 2.7 fusion.62
  373.7 1.1 slice.156
  375.2 1.1 all_to_all.58
  376.2 3.5 all-to-all-start.2
  380.1 1.1 all_to_all.61
  381.3 5.3 %all-to-all-done.2 = bf16[8,64,384]{2,1,0:T(8,128)(2,1)S(1)} async-done(((bf16[8,64,384]{2,1,0:T(8,128)(2,1)}), bf16[8,64,384]{2,1,0:T(8,128)(2,1)S(1)}, u32[]{:S(2)}, u32[]{:S(2)}) %all-to-all-start.2) | async-done | bytes 393248 | tf_op jit(solution)/shard_map/all_to_all | solution.py:134
  386.5 3.5 all-to-all-start.3
  391.2 5.9 %all-to-all-done.3 = bf16[8,72,384]{2,1,0:T(8,128)(2,1)S(1)} async-done(((bf16[8,72,384]{2,1,0:T(8,128)(2,1)}), bf16[8,72,384]{2,1,0:T(8,128)(2,1)S(1)}, u32[]{:S(2)}, u32[]{:S(2)}) %all-to-all-start.3) | async-done | bytes 442400 | tf_op jit(solution)/shard_map/all_to_all | solution.py:135
  397.1 1.0 broadcast_in_dim.22
  (100 shorter events, 26.1 us)
Async XLA Ops:
  7.2 128.1 %all-gather.11.cloned.1.call-start = ((), (), s32[]{:S(2)}) async-start(), calls=%async_computation.7 | async-start | bytes 7299072 | tf_op jit(solution)/shard_map/all_gather | solution.py:111
  34.7 197.0 %all-gather.7.cloned.1.call-start = ((), (), s32[]{:S(2)}) async-start(), calls=%async_computation.5 | async-start | bytes 7299072 | tf_op jit(solution)/shard_map/all_gather | solution.py:111
  54.9 11.2 %copy-start.1 = (bf16[1,64,3072]{2,1,0:T(8,128)(2,1)S(1)}, bf16[1,64,3072]{2,1,0:T(8,128)(2,1)}, u32[]{:S(2)}) copy-start(bf16[1,64,3072]{2,1,0:T(8,128)(2,1)} %param.9) | copy-start | bytes 1179652
  58.0 7.1 %copy-start = (bf16[1,72,3072]{2,1,0:T(8,128)(2,1)S(1)}, bf16[1,72,3072]{2,1,0:T(8,128)(2,1)}, u32[]{:S(2)}) copy-start(bf16[1,72,3072]{2,1,0:T(8,128)(2,1)} %param.10) | copy-start | bytes 1327108
  59.7 219.4 %all-gather.9.cloned.1.call-start = ((), (), s32[]{:S(2)}) async-start(), calls=%async_computation.6 | async-start | bytes 3981312 | tf_op jit(solution)/shard_map/all_gather | solution.py:112
  64.9 5.8 %copy-start.12 = (f32[2,2,128]{2,1,0:T(2,128)S(1)}, f32[2,2,128]{2,1,0:T(2,128)}, u32[]{:S(2)}) copy-start(f32[2,2,128]{2,1,0:T(2,128)} %param.12) | copy-start | bytes 6148
  66.0 258.9 %all-gather.5.cloned.1.call-start = ((), (), s32[]{:S(2)}) async-start(), calls=%async_computation.4 | async-start | bytes 3538944 | tf_op jit(solution)/shard_map/all_gather | solution.py:112
  337.3 0.9 copy-start.8
  338.2 4.8 %copy-start.3 = (f32[512,1,3,128]{0,3,2,1:T(8,128)S(1)}, f32[512,1,3,128]{0,3,2,1:T(8,128)}, u32[]{:S(2)}) copy-start(f32[512,1,3,128]{0,3,2,1:T(8,128)} %get-tuple-element.92) | copy-start | bytes 2359300
  338.2 5.9 %copy-start.2 = (f32[512,1,3,128]{0,3,2,1:T(8,128)S(1)}, f32[512,1,3,128]{0,3,2,1:T(8,128)}, u32[]{:S(2)}) copy-start(f32[512,1,3,128]{0,3,2,1:T(8,128)} %get-tuple-element.93) | copy-start | bytes 2359300
  341.5 3.1 copy-start.11
  343.0 3.0 copy-start.9
  344.6 1.5 copy-start.10
  349.1 2.0 copy-start.4
  352.3 5.3 %copy-start.6 = (bf16[512,3,128]{0,2,1:T(8,128)(2,1)S(1)}, bf16[512,3,128]{0,2,1:T(8,128)(2,1)}, u32[]{:S(2)}) copy-start(bf16[512,3,128]{0,2,1:T(8,128)(2,1)} %fusion.36) | copy-start | bytes 1179652
  352.7 5.2 %copy-start.5 = (bf16[576,3,128]{2,0,1:T(8,128)(2,1)S(1)}, bf16[576,3,128]{2,0,1:T(8,128)(2,1)}, u32[]{:S(2)}) copy-start(bf16[576,3,128]{2,0,1:T(8,128)(2,1)} %fusion.35) | copy-start | bytes 1327108
  373.7 6.0 %copy-start.7 = (bf16[3,1088,128]{2,1,0:T(8,128)(2,1)S(1)}, bf16[3,1088,128]{2,1,0:T(8,128)(2,1)}, u32[]{:S(2)}) copy-start(bf16[3,1088,128]{2,1,0:T(8,128)(2,1)} %get-tuple-element.34) | copy-start | bytes 2506756
  376.2 10.3 %all-to-all-start.2 = ((bf16[8,64,384]{2,1,0:T(8,128)(2,1)}), bf16[8,64,384]{2,1,0:T(8,128)(2,1)S(1)}, u32[]{:S(2)}, u32[]{:S(2)}) async-start(bf16[8,64,384]{2,1,0:T(8,128)(2,1)} %all_to_all.58), calls=%async_computation.2 | async-start | bytes 786432 | tf_op jit(solution)/shard_map/all_to_all | solution.py:134
  386.5 10.5 %all-to-all-start.3 = ((bf16[8,72,384]{2,1,0:T(8,128)(2,1)}), bf16[8,72,384]{2,1,0:T(8,128)(2,1)S(1)}, u32[]{:S(2)}, u32[]{:S(2)}) async-start(bf16[8,72,384]{2,1,0:T(8,128)(2,1)} %all_to_all.61), calls=%async_computation.3 | async-start | bytes 884736 | tf_op jit(solution)/shard_map/all_to_all | solution.py:135
Sparse Core Ops, SparseCore 0:
  34.8 100.4 all-gather.10
  138.1 93.5 all-gather.6
  234.1 45.0 all-gather.8
  281.4 43.5 all-gather.4
where the time goes:
time: 410 us; the launch traced here: 405 us
  waiting for transfers between devices  234 us (57%)
  local copies, waits for them, and re-layouts  70.9 us (17%)
  other arithmetic  31.5 us (8%)
  matrix products  25.2 us (6%)
  blocking collectives  20.9 us (5%)
  between operations  15 us (4%)
  starting transfers between devices  7.09 us (2%)
    all_gather x2, waiting for transfers between devices, on_device(): full_weight = lax.all_gather(relaid, 'rep', axis=0, tiled=True)  149 us
    all_gather x2, waiting for transfers between devices, on_device(): all_rows = lax.all_gather(modded, 'seq', axis=0, tiled=True)  73.3 us
    all_to_all x2, blocking collectives, on_device(): lax.all_to_all(weights[stream], 'seq', split_axis=2, concat_axis=0, tiled...  20.9 us
    all_gather x2, local copies, waits for them, and re-layouts, on_device(): full_weight = lax.all_gather(relaid, 'rep', axis=0, tiled=True)  20.5 us
    unnamed x32, local copies, waits for them, and re-layouts  15.6 us
    dot_general x2, matrix products, on_device(): jnp.dot(all_rows, full_weight.reshape(D, 3 * col_count), preferred_elemen...  14.6 us
    squeeze x3, local copies, waits for them, and re-layouts, on_device(): weights[stream]  8.49 us
  transfers between devices with their start and end apart: 6, of which 6 were waited for; matrix products, arithmetic and copies ran while one was open for 14% of the time, Pallas kernels for 0%

commit v1 on v0

v1 whole, which is shorter than its diff:
```python
import functools

import jax
import jax.numpy as jnp
import numpy as np
from jax import lax
from jax.experimental import pallas as pl
from jax.experimental.pallas import tpu as pltpu
from jax.sharding import PartitionSpec as P

D = 3072
HD = 128
GRID = 24
TXT = 512
IMG = GRID * GRID
TOTAL = TXT + IMG
SEQ = 8
NZ = 8
HEADS_HERE = 3
TROWS = TXT // SEQ
IROWS = IMG // SEQ
REST = IROWS - 64
WROWS = 12
KSTEP = 768
SCALE = float(HD**-0.5 * np.log2(np.e))
MESH = pl.DeviceIdType.MESH
BF16, F32 = jnp.bfloat16, jnp.float32


def rope_rows():
    pairs, still = HD // 2, HD // 16
    rows = (pairs - still) // 2
    cols = pairs - still - rows
    place = np.concatenate(
        [
            (np.arange(SEQ)[:, None] * IROWS + np.arange(64)[None, :]).reshape(-1),
            (np.arange(SEQ)[:, None] * IROWS + 64 + np.arange(REST)[None, :]).reshape(-1),
        ]
    )
    row_pos = (place // GRID).astype(np.float32)
    col_pos = (place % GRID).astype(np.float32)
    row_freq = (10000.0 ** (-np.arange(rows) / rows)).astype(np.float32)
    col_freq = (10000.0 ** (-np.arange(cols) / cols)).astype(np.float32)
    angles = np.concatenate(
        [
            np.zeros((IMG, still), np.float32),
            row_pos[:, None] * row_freq[None, :],
            col_pos[:, None] * col_freq[None, :],
        ],
        axis=1,
    )
    cosine = np.repeat(np.cos(angles), 2, axis=1)
    sine = np.repeat(np.sin(angles), 2, axis=1)
    sine[:, 0::2] *= -1.0
    return cosine.astype(np.float32), sine.astype(np.float32)


def kernel(
    wsrc, text, image, mods, gains, cosine, sine, length,
    out,
    W, A, T, RM, XR, acc, Q, K, V, OB, bias, sel,
    a2a_s, a2a_r, y_s, y_r, zr_s, zr_r, zl_s, zl_r, sib_s, sib_r, tok_s, tok_r, out_s, out_r, own_sem,
):
    R, S = lax.axis_index("rep"), lax.axis_index("seq")
    core = lax.rem(R, 2)
    z = lax.rem(R // 2, NZ)
    yh = R // (2 * NZ)
    x = lax.rem(S, 4)
    yl = S // 4

    def rep_of(y, zz, c):
        return (y * NZ + zz) * 2 + c

    def up(dz):
        return lax.rem(z + dz + NZ, NZ)

    def xs(dx, row):
        return row * 4 + lax.rem(x + dx + 4, 4)

    sib = (rep_of(yh, z, 1 - core), S)
    zr = (rep_of(yh, up(1), core), S)
    zl = (rep_of(yh, up(-1), core), S)
    yp = (rep_of(1 - yh, z, core), S)
    peers = [(R, lax.rem(S + d, SEQ)) for d in range(1, SEQ)]
    s_yp, s_xr, s_xl, s_xx = xs(0, 1 - yl), xs(1, yl), xs(-1, yl), xs(2, yl)
    o_xr, o_xl, o_xx = xs(1, 1 - yl), xs(-1, 1 - yl), xs(2, 1 - yl)

    barrier = pltpu.get_barrier_semaphore()
    partners = [sib, zr, zl, yp] + peers
    for device in partners:
        pl.semaphore_signal(barrier, inc=1, device_id=device, device_id_type=MESH)
    pl.semaphore_wait(barrier, len(partners))

    pending = []

    def send(src, dst, ssem, rsem, device):
        copy = pltpu.make_async_remote_copy(
            src_ref=src, dst_ref=dst, send_sem=ssem, recv_sem=rsem, device_id=device, device_id_type=MESH
        )
        copy.start()
        pending.append(copy)

    def arrived(dst, ssem, rsem, device):
        pltpu.make_async_remote_copy(
            src_ref=dst, dst_ref=dst, send_sem=ssem, recv_sem=rsem, device_id=device, device_id_type=MESH
        ).wait_recv()

    def slot(j, s):
        return A.at[j, :, :, pl.ds(pl.multiple_of(s * 16, 16), 16), :]

    def piece(j, g):
        return wsrc.at[:, :, :, pl.ds(pl.multiple_of(g * (HEADS_HERE * HD) + j * HD, HD), HD)]

    def a2a_start(j):
        for d in range(1, SEQ):
            send(piece(j, peers[d - 1][1]), slot(j, S), a2a_s.at[j, d - 1], a2a_r.at[j, d - 1], peers[d - 1])
        copy = pltpu.make_async_copy(piece(j, S), slot(j, S), own_sem.at[j])
        copy.start()
        return copy

    own_copies = [a2a_start(0)]

    def modulate(rows, stream):
        v = rows.astype(F32)
        center = v - jnp.mean(v, axis=-1, keepdims=True)
        spread = jnp.mean(center * center, axis=-1, keepdims=True)
        normed = center * lax.rsqrt(spread + 1e-06)
        return normed * (1.0 + mods[2 * stream + 1 : 2 * stream + 2, :]) + mods[2 * stream : 2 * stream + 1, :]

    def mod_text(i, carry):
        rows = pl.ds(pl.multiple_of(i * 16, 16), 16)
        T[S, rows, :] = modulate(text[rows, :], 0).astype(BF16)
        return carry

    def mod_image(i, carry):
        rows = pl.ds(pl.multiple_of(i * 16, 16), 16)
        T[S, pl.ds(pl.multiple_of(64 + i * 16, 16), 16), :] = modulate(image[rows, :], 1).astype(BF16)
        return carry

    lax.fori_loop(0, 4, mod_text, 0)
    lax.fori_loop(0, 4, mod_image, 0)
    rest = modulate(image[64:72, :], 1)
    RM[S] = jnp.concatenate([rest[:, : D // 2], rest[:, D // 2 :]], axis=0).astype(BF16)

    def send_tokens(s, first, device):
        send(T.at[s], T.at[s], tok_s.at[first], tok_r.at[first], device)
        send(RM.at[s], RM.at[s], tok_s.at[first + 1], tok_r.at[first + 1], device)

    def tokens_arrived(s, first, device):
        arrived(T.at[s], tok_s.at[first], tok_r.at[first], device)
        arrived(RM.at[s], tok_s.at[first + 1], tok_r.at[first + 1], device)

    d_yp, d_xr, d_xl = (R, s_yp), (R, s_xr), (R, s_xl)
    send_tokens(S, 0, d_xr)
    send_tokens(S, 2, d_xl)
    send_tokens(S, 4, d_yp)
    own_copies.append(a2a_start(1))
    own_copies.append(a2a_start(2))

    i96 = lax.broadcasted_iota(jnp.int32, (96, 128), 0)
    i128 = lax.broadcasted_iota(jnp.int32, (96, 128), 1)
    sel[...] = jnp.where(i128 == (i96 // WROWS) * 16 + lax.rem(i96, WROWS), 1.0, 0.0).astype(BF16)
    where = lax.broadcasted_iota(jnp.int32, (8, TXT), 1)
    bias[...] = jnp.where(where < length[0], 0.0, -jnp.inf).astype(F32)

    def rows_of(zz, c):
        return pl.ds(pl.multiple_of((zz * 2 + c) * 96, 32), 96)

    def block(j, y, zz, c):
        return W.at[j, :, y, rows_of(zz, c), :]

    def half(j, st, y, zz, c):
        return W.at[j, st, y, rows_of(zz, c), :]

    def gather_rows(j):
        own_copies[j].wait()
        for d in range(1, SEQ):
            src = lax.rem(S + SEQ - d, SEQ)
            arrived(slot(j, src), a2a_s.at[j, d - 1], a2a_r.at[j, d - 1], peers[d - 1])
        for st in range(2):
            rows = jnp.concatenate([A[j, st, q] for q in range(3)], axis=1)
            W[j, st, yh, rows_of(z, core), :] = jnp.dot(sel[...], rows, preferred_element_type=F32).astype(BF16)

    yy = [yh, 1 - yh]

    def sib_send(j, w, k, zz):
        b = block(j, yy[w], zz, core)
        send(b, b, sib_s.at[j, w, k], sib_r.at[j, w, k], sib)

    def begin(j):
        gather_rows(j)
        b = block(j, yh, z, core)
        send(b, b, y_s.at[j], y_r.at[j], yp)
        send(b, b, zr_s.at[j, 0, 0], zr_r.at[j, 0, 0], zr)
        send(b, b, zl_s.at[j, 0, 0], zl_r.at[j, 0, 0], zl)
        sib_send(j, 0, 0, z)

    def begin_partner(j):
        b = block(j, 1 - yh, z, core)
        arrived(b, y_s.at[j], y_r.at[j], yp)
        send(b, b, zr_s.at[j, 1, 0], zr_r.at[j, 1, 0], zr)
        send(b, b, zl_s.at[j, 1, 0], zl_r.at[j, 1, 0], zl)
        sib_send(j, 1, 0, z)

    def hop(j, w, step):
        y = yy[w]
        if step < 4:
            b = block(j, y, up(-step), core)
            arrived(b, zr_s.at[j, w, step - 1], zr_r.at[j, w, step - 1], zr)
            f = b if step < 3 else half(j, 0, y, up(-step), core)
            send(f, f, zr_s.at[j, w, step], zr_r.at[j, w, step], zr)
            sib_send(j, w, step, up(-step))
            b = block(j, y, up(step), core)
            arrived(b, zl_s.at[j, w, step - 1], zl_r.at[j, w, step - 1], zl)
            f = b if step < 3 else half(j, 1, y, up(step), core)
            send(f, f, zl_s.at[j, w, step], zl_r.at[j, w, step], zl)
            sib_send(j, w, step + 3, up(step))
        else:
            arrived(half(j, 0, y, up(4), core), zr_s.at[j, w, 3], zr_r.at[j, w, 3], zr)
            arrived(half(j, 1, y, up(4), core), zl_s.at[j, w, 3], zl_r.at[j, w, 3], zl)
            sib_send(j, w, 7, up(4))

    def sib_arrived(j):
        for w in range(2):
            for k, dz in enumerate((0, -1, -2, -3, 1, 2, 3, 4)):
                arrived(block(j, yy[w], up(dz), 1 - core), sib_s.at[j, w, k], sib_r.at[j, w, k], sib)

    def project(j, st):
        n = TXT if st == 0 else IMG
        acc[0:n, :] = jnp.zeros((n, 3 * HD), F32)

        def body(k, carry):
            cols = pl.ds(pl.multiple_of(k * KSTEP, KSTEP), KSTEP)
            lhs = T[:, 64 * st : 64 * st + 64, cols].reshape(SEQ * 64, KSTEP)
            if st == 1:
                lhs = jnp.concatenate([lhs, XR[:, cols]], axis=0)
            rhs = W[j, st, k // 2, pl.ds(pl.multiple_of(lax.rem(k, 2) * KSTEP, KSTEP), KSTEP), :]
            acc[0:n, :] += jnp.dot(lhs, rhs, preferred_element_type=F32)
            return carry

        lax.fori_loop(0, D // KSTEP, body, 0)

    even = lax.rem(lax.broadcasted_iota(jnp.int32, (64, HD), 1), 2) == 0

    def finish(st):
        base = 0 if st == 0 else TXT

        def body(i, carry):
            here = pl.ds(pl.multiple_of(i * 64, 64), 64)
            there = pl.ds(pl.multiple_of(base + i * 64, 64), 64)
            for part, store in ((0, Q), (1, K)):
                v = acc[here, part * HD : (part + 1) * HD]
                power = jnp.mean(v * v, axis=-1, keepdims=True)
                v = v * lax.rsqrt(power + 1e-06) * gains[2 * st + part : 2 * st + part + 1, :]
                if st == 1:
                    turned = jnp.where(even, pltpu.roll(v, HD - 1, 1), pltpu.roll(v, 1, 1))
                    v = v * cosine[here, :] + turned * sine[here, :]
                store[there, :] = v.astype(BF16)
            V[there, :] = acc[here, 2 * HD : 3 * HD].astype(BF16)
            return carry

        lax.fori_loop(0, (TXT if st == 0 else IMG) // 64, body, 0)

    def attend(q):
        scores = lax.dot_general(q, K[...], (((1,), (1,)), ((), ())), preferred_element_type=F32) * SCALE
        scores = jnp.concatenate([scores[:, :TXT] + bias[0:1, :], scores[:, TXT:]], axis=1)
        weight = jnp.exp2(scores - jnp.max(scores, axis=-1, keepdims=True))
        total = jnp.sum(weight, axis=-1, keepdims=True)
        return jnp.dot(weight.astype(BF16), V[...], preferred_element_type=F32) / total

    def attend_full(j, st):
        def body(i, carry):
            o = attend(Q[pl.ds(pl.multiple_of(st * 512 + i * 256, 256), 256), :])
            OB[j, pl.ds(i * 4, 4), 64 * st : 64 * st + 64, :] = o.astype(BF16).reshape(4, 64, HD)
            return carry

        lax.fori_loop(0, 2, body, 0)

    def attend_rest(j):
        o = attend(Q[1024:1088, :]).reshape(SEQ, REST, HD)
        OB[j, :, 128:144, :] = jnp.concatenate([o, jnp.zeros_like(o)], axis=1).astype(BF16)

    def give(j):
        lanes = pl.ds(pl.multiple_of((S * HEADS_HERE + j) * HD, HD), HD)
        for d in range(1, SEQ):
            send(OB.at[j, peers[d - 1][1]], out.at[:, lanes], out_s.at[j, d - 1], out_r.at[j, d - 1], peers[d - 1])
        out[:, lanes] = OB[j, S]

    def take(j):
        for d in range(1, SEQ):
            src = lax.rem(S + SEQ - d, SEQ)
            lanes = pl.ds(pl.multiple_of((src * HEADS_HERE + j) * HD, HD), HD)
            arrived(out.at[:, lanes], out_s.at[j, d - 1], out_r.at[j, d - 1], peers[d - 1])

    def parts_of(j):
        return [
            lambda: (sib_arrived(j), project(j, 0), finish(0)),
            lambda: (project(j, 1), finish(1)),
            lambda: attend_full(j, 0),
            lambda: (attend_full(j, 1), attend_rest(j), give(j)),
        ]

    begin(0)
    begin_partner(0)
    for step in (1, 2):
        for w in (0, 1):
            hop(0, w, step)
    tokens_arrived(s_xl, 0, d_xr)
    send(T.at[s_xl, 0:64], T.at[s_xl, 0:64], tok_s.at[6], tok_r.at[6], d_xr)
    tokens_arrived(s_xr, 2, d_xl)
    send(T.at[s_xr, 64:128], T.at[s_xr, 64:128], tok_s.at[7], tok_r.at[7], d_xl)
    send(RM.at[s_xr], RM.at[s_xr], tok_s.at[8], tok_r.at[8], d_xl)
    tokens_arrived(s_yp, 4, d_yp)
    send_tokens(s_yp, 9, d_xr)
    send_tokens(s_yp, 11, d_xl)
    for w in (0, 1):
        hop(0, w, 3)
    begin(1)
    begin_partner(1)
    for w in (0, 1):
        hop(0, w, 4)
    for w in (0, 1):
        hop(1, w, 1)
    arrived(T.at[s_xx, 0:64], tok_s.at[6], tok_r.at[6], d_xr)
    arrived(T.at[s_xx, 64:128], tok_s.at[7], tok_r.at[7], d_xl)
    arrived(RM.at[s_xx], tok_s.at[8], tok_r.at[8], d_xl)
    send_tokens(s_xx, 13, d_yp)
    for step in (2, 3):
        for w in (0, 1):
            hop(1, w, step)
    begin(2)
    begin_partner(2)
    tokens_arrived(o_xl, 9, d_xr)
    tokens_arrived(o_xr, 11, d_xl)
    tokens_arrived(o_xx, 13, d_yp)

    def unpack(i, carry):
        pair = [RM[2 * i + n].astype(F32) for n in range(2)]
        rows = [jnp.concatenate([p[0:8], p[8:16]], axis=1) for p in pair]
        XR[pl.ds(pl.multiple_of(i * 16, 16), 16), :] = jnp.concatenate(rows, axis=0).astype(BF16)
        return carry

    lax.fori_loop(0, 4, unpack, 0)
    for w in (0, 1):
        hop(1, w, 4)
    todo = parts_of(0) + parts_of(1)
    for step in (1, 2, 3, 4):
        for w in (0, 1):
            if todo:
                todo.pop(0)()
            hop(2, w, step)
    for part in todo + parts_of(2):
        part()
    for j in range(HEADS_HERE):
        take(j)
    for copy in pending:
        copy.wait_send()


def on_device(text_tokens, image_tokens, weights, qk_gain, mod_table, text_lengths, time_index):
    mods = lax.dynamic_index_in_dim(mod_table, time_index[0], 0, keepdims=False).reshape(4, D)
    wsrc = jnp.pad(jnp.swapaxes(weights, 1, 2), ((0, 0), (0, 0), (0, 16 - WROWS), (0, 0)))
    cosine, sine = rope_rows()
    vmem = pl.BlockSpec(memory_space=pltpu.VMEM)
    dma = pltpu.SemaphoreType.DMA
    n_tok = 15
    result = pl.pallas_call(
        kernel,
        out_shape=jax.ShapeDtypeStruct((144, D), BF16),
        in_specs=[vmem] * 7 + [pl.BlockSpec(memory_space=pltpu.SMEM)],
        out_specs=vmem,
        scratch_shapes=[
            pltpu.VMEM((HEADS_HERE, 2, 2, D // 2, 3 * HD), BF16),
            pltpu.VMEM((HEADS_HERE, 2, 3, 128, HD), BF16),
            pltpu.VMEM((SEQ, 128, D), BF16),
            pltpu.VMEM((SEQ, 16, D // 2), BF16),
            pltpu.VMEM((SEQ * REST, D), BF16),
            pltpu.VMEM((IMG, 3 * HD), F32),
            pltpu.VMEM((TOTAL, HD), BF16),
            pltpu.VMEM((TOTAL, HD), BF16),
            pltpu.VMEM((TOTAL, HD), BF16),
            pltpu.VMEM((HEADS_HERE, SEQ, 144, HD), BF16),
            pltpu.VMEM((8, TXT), F32),
            pltpu.VMEM((96, 128), BF16),
            dma((3, 7)), dma((3, 7)),
            dma((3,)), dma((3,)),
            dma((3, 2, 4)), dma((3, 2, 4)),
            dma((3, 2, 4)), dma((3, 2, 4)),
            dma((3, 2, 8)), dma((3, 2, 8)),
            dma((n_tok,)), dma((n_tok,)),
            dma((3, 7)), dma((3, 7)),
            dma((3,)),
        ],
        compiler_params=pltpu.CompilerParams(
            collective_id=0, has_side_effects=True, vmem_limit_bytes=56 * 1024 * 1024
        ),
        cost_estimate=pl.CostEstimate(flops=9_500_000_000, bytes_accessed=30_000_000, transcendentals=3_600_000),
        name="joint_attention",
    )(
        wsrc, text_tokens[0], image_tokens[0], mods, qk_gain.reshape(4, HD),
        jnp.asarray(cosine), jnp.asarray(sine), text_lengths.astype(jnp.int32),
    )
    return result[None, :TROWS], result[None, TROWS : TROWS + IROWS]


def solution(mesh):
    placed = (
        P("rep", "seq", None),
        P("rep", "seq", None),
        P(None, ("rep", "seq"), None, None),
        P(),
        P(),
        P("rep"),
        P("rep"),
    )
    return jax.shard_map(
        on_device,
        mesh=mesh,
        in_specs=placed,
        out_specs=(P("rep", "seq", None), P("rep", "seq", None)),
        check_vma=False,
    )
```

time: 410 us -> 146 us (0.36); the launches traced: 405 us -> 146 us
  waiting for transfers between devices: 234 us -> 0 us
  Pallas kernels: 0 us -> 138 us
  local copies, waits for them, and re-layouts: 70.9 us -> 6.24 us
  other arithmetic: 31.5 us -> 0 us
  matrix products: 25.2 us -> 0 us
  blocking collectives: 20.9 us -> 0 us
  between operations: 15 us -> 2.07 us
  starting transfers between devices: 7.09 us -> 0 us
    all_gather x4 -> x0, waiting for transfers between devices: 223 us -> none  [the longest x2 149 us: on_device(): full_weight = lax.all_gather(relaid, 'rep', axis=0, tiled=True)]
    pallas_call x0 -> x1, Pallas kernels: none -> 138 us  [on_device(): pl.pallas_call(kernel, out_shape=jax.ShapeDtypeStruct((144, D), BF16), in...]
    dot_general x8 -> x0, matrix products: 25.2 us -> none  [the longest x2 14.6 us: on_device(): jnp.dot(all_rows, full_weight.reshape(D, 3 * col_count), preferred_elemen...]
    all_to_all x2 -> x0, blocking collectives: 20.9 us -> none  [on_device(): lax.all_to_all(weights[stream], 'seq', split_axis=2, concat_axis=0, tiled...]
    all_gather x2 -> x0, local copies, waits for them, and re-layouts: 20.5 us -> none  [on_device(): full_weight = lax.all_gather(relaid, 'rep', axis=0, tiled=True)]
    unnamed x32 -> x3, local copies, waits for them, and re-layouts: 15.6 us -> 1.11 us
    another operation x6 -> x0, other arithmetic: 11.6 us -> none
    all_to_all x2 -> x0, waiting for transfers between devices: 11.1 us -> none  [the longest x1 5.87 us: on_device(): lax.all_to_all(joined[TXT:], 'seq', split_axis=0, concat_axis=1, tiled=True)]
  transfers between devices with their start and end apart: 6 -> 0, of which waited for: 6 -> 0; matrix products, arithmetic and copies ran while one was open for 14% -> 0% of each run, Pallas kernels for 0% -> 0%
where the time goes in v1:
time: 146 us
  Pallas kernels  138 us (95%)
  local copies, waits for them, and re-layouts  6.24 us (4%)
  between operations  2.07 us (1%)
    pallas_call x1, Pallas kernels, on_device(): pl.pallas_call(kernel, out_shape=jax.ShapeDtypeStruct((144, D), BF16), in...  138 us
    broadcast_in_dim x2, local copies, waits for them, and re-layouts, on_device(): return (result[None, :TROWS], result[None, TROWS:TROWS + IROWS])  3.57 us

profile of v1, /device:TPU:1, one launch (start us, length us, event | category | flops | bytes accessed | tf_op | source)
XLA Modules:
  0.0 146.2 jit_solution(8762566268518739170)
XLA Ops:
  0.6 0.0 copy-start
  2.0 0.0 copy-done
  2.1 0.7 reshape.11.mods
  2.7 1.1 copy.13
  3.9 0.9 pad.4.wsrc
  4.7 137.9 %joint_attention.1 = bf16[144,3072]{1,0:T(8,128)(2,1)} custom-call(bf16[2,3,16,3072]{3,2,1,0:T(8,128)(2,1)} %pad.4.wsrc, bf16[64,3072]{1,0:T(8,128)(2,1)} %bitcast.16, bf16[72,3072]{1,0:T(8,128)(2,1)} %bitcast.15, f32[4,3072]{1,0:T(4,128)} %reshape.11.mods, f32[4,128]{1,0:T(4,128)} %bitcast.17, f32[576,128]{1,0:T(8,128)} %constant.13.clone.cosine, ...), custom_call_target="tpu_custom_call" | custom-call | flops 9500000256 | bytes 30000000 | tf_op jit(solution)/shard_map/joint_attention/pallas_call | solution.py:367
  142.6 1.8 %slice_bitcast_fusion.1 = bf16[1,64,3072]{2,1,0:T(8,128)(2,1)} fusion(bf16[144,3072]{1,0:T(8,128)(2,1)} %joint_attention.1), kind=kLoop, calls=%fused_computation.2 | loop fusion | bytes 786432 | tf_op jit(solution)/shard_map/broadcast_in_dim | solution.py:403
  144.4 1.8 %slice_bitcast_fusion = bf16[1,72,3072]{2,1,0:T(8,128)(2,1)} fusion(bf16[144,3072]{1,0:T(8,128)(2,1)} %joint_attention.1), kind=kLoop, calls=%fused_computation.1 | loop fusion | bytes 884736 | tf_op jit(solution)/shard_map/broadcast_in_dim | solution.py:403
  (1 shorter events, 0.0 us)
Async XLA Ops:
  0.6 1.4 copy-start

commit v2 on v1

--- a/solution.py
+++ b/solution.py
@@ -56,9 +56,9 @@
 
 
 def kernel(
-    wsrc, text, image, mods, gains, cosine, sine, length,
+    wraw, text, image, mods, gains, cosine, sine, length,
     out,
-    W, A, T, RM, XR, acc, Q, K, V, OB, bias, sel,
+    wsrc, W, A, T, RM, XR, Q, K, V, OB, bias, sel,
     a2a_s, a2a_r, y_s, y_r, zr_s, zr_r, zl_s, zl_r, sib_s, sib_r, tok_s, tok_r, out_s, out_r, own_sem,
 ):
     R, S = lax.axis_index("rep"), lax.axis_index("seq")
@@ -85,6 +85,9 @@
     s_yp, s_xr, s_xl, s_xx = xs(0, 1 - yl), xs(1, yl), xs(-1, yl), xs(2, yl)
     o_xr, o_xl, o_xx = xs(1, 1 - yl), xs(-1, 1 - yl), xs(2, 1 - yl)
 
+    wsrc[:, :, 0:WROWS, :] = wraw[...]
+    wsrc[:, :, WROWS:16, :] = jnp.zeros((2, 3, 16 - WROWS, D), BF16)
+
     barrier = pltpu.get_barrier_semaphore()
     partners = [sib, zr, zl, yp] + peers
     for device in partners:
@@ -125,7 +128,7 @@
         center = v - jnp.mean(v, axis=-1, keepdims=True)
         spread = jnp.mean(center * center, axis=-1, keepdims=True)
         normed = center * lax.rsqrt(spread + 1e-06)
-        return normed * (1.0 + mods[2 * stream + 1 : 2 * stream + 2, :]) + mods[2 * stream : 2 * stream + 1, :]
+        return normed * (1.0 + mods[stream, 1:2, :]) + mods[stream, 0:1, :]
 
     def mod_text(i, carry):
         rows = pl.ds(pl.multiple_of(i * 16, 16), 16)
@@ -150,13 +153,9 @@
         arrived(T.at[s], tok_s.at[first], tok_r.at[first], device)
         arrived(RM.at[s], tok_s.at[first + 1], tok_r.at[first + 1], device)
 
-    d_yp, d_xr, d_xl = (R, s_yp), (R, s_xr), (R, s_xl)
-    send_tokens(S, 0, d_xr)
-    send_tokens(S, 2, d_xl)
-    send_tokens(S, 4, d_yp)
     own_copies.append(a2a_start(1))
     own_copies.append(a2a_start(2))
-
+    d_yp, d_xr, d_xl = (R, s_yp), (R, s_xr), (R, s_xl)
     i96 = lax.broadcasted_iota(jnp.int32, (96, 128), 0)
     i128 = lax.broadcasted_iota(jnp.int32, (96, 128), 1)
     sel[...] = jnp.where(i128 == (i96 // WROWS) * 16 + lax.rem(i96, WROWS), 1.0, 0.0).astype(BF16)
@@ -226,59 +225,37 @@
                 arrived(block(j, yy[w], up(dz), 1 - core), sib_s.at[j, w, k], sib_r.at[j, w, k], sib)
 
     def project(j, st):
-        n = TXT if st == 0 else IMG
-        acc[0:n, :] = jnp.zeros((n, 3 * HD), F32)
-
-        def body(k, carry):
-            cols = pl.ds(pl.multiple_of(k * KSTEP, KSTEP), KSTEP)
-            lhs = T[:, 64 * st : 64 * st + 64, cols].reshape(SEQ * 64, KSTEP)
+        n, base = (TXT, 0) if st == 0 else (IMG, TXT)
+        lhs = T[:, 64 * st : 64 * st + 64, :].reshape(SEQ * 64, D)
+        if st == 1:
+            lhs = jnp.concatenate([lhs, XR[...]], axis=0)
+        rows = jnp.dot(lhs, W[j, st].reshape(D, 3 * HD), preferred_element_type=F32)
+        for part, store in ((0, Q), (1, K)):
+            v = rows[:, part * HD : (part + 1) * HD]
+            power = jnp.mean(v * v, axis=-1, keepdims=True)
+            v = v * lax.rsqrt(power + 1e-06) * gains[2 * st + part : 2 * st + part + 1, :]
             if st == 1:
-                lhs = jnp.concatenate([lhs, XR[:, cols]], axis=0)
-            rhs = W[j, st, k // 2, pl.ds(pl.multiple_of(lax.rem(k, 2) * KSTEP, KSTEP), KSTEP), :]
-            acc[0:n, :] += jnp.dot(lhs, rhs, preferred_element_type=F32)
-            return carry
-
-        lax.fori_loop(0, D // KSTEP, body, 0)
-
-    even = lax.rem(lax.broadcasted_iota(jnp.int32, (64, HD), 1), 2) == 0
-
-    def finish(st):
-        base = 0 if st == 0 else TXT
-
-        def body(i, carry):
-            here = pl.ds(pl.multiple_of(i * 64, 64), 64)
-            there = pl.ds(pl.multiple_of(base + i * 64, 64), 64)
-            for part, store in ((0, Q), (1, K)):
-                v = acc[here, part * HD : (part + 1) * HD]
-                power = jnp.mean(v * v, axis=-1, keepdims=True)
-                v = v * lax.rsqrt(power + 1e-06) * gains[2 * st + part : 2 * st + part + 1, :]
-                if st == 1:
-                    turned = jnp.where(even, pltpu.roll(v, HD - 1, 1), pltpu.roll(v, 1, 1))
-                    v = v * cosine[here, :] + turned * sine[here, :]
-                store[there, :] = v.astype(BF16)
-            V[there, :] = acc[here, 2 * HD : 3 * HD].astype(BF16)
-            return carry
-
-        lax.fori_loop(0, (TXT if st == 0 else IMG) // 64, body, 0)
-
-    def attend(q):
-        scores = lax.dot_general(q, K[...], (((1,), (1,)), ((), ())), preferred_element_type=F32) * SCALE
+                even = lax.rem(lax.broadcasted_iota(jnp.int32, (n, HD), 1), 2) == 0
+                turned = jnp.where(even, pltpu.roll(v, HD - 1, 1), pltpu.roll(v, 1, 1))
+                v = v * cosine[...] + turned * sine[...]
+            store[base : base + n, :] = v.astype(BF16)
+        V[base : base + n, 0:HD] = rows[:, 2 * HD : 3 * HD].astype(BF16)
+
+    def attend_rows(q):
+        scores = lax.dot_general(q, K[...], (((1,), (1,)), ((), ())), preferred_element_type=F32)
         scores = jnp.concatenate([scores[:, :TXT] + bias[0:1, :], scores[:, TXT:]], axis=1)
-        weight = jnp.exp2(scores - jnp.max(scores, axis=-1, keepdims=True))
-        total = jnp.sum(weight, axis=-1, keepdims=True)
-        return jnp.dot(weight.astype(BF16), V[...], preferred_element_type=F32) / total
-
-    def attend_full(j, st):
-        def body(i, carry):
-            o = attend(Q[pl.ds(pl.multiple_of(st * 512 + i * 256, 256), 256), :])
-            OB[j, pl.ds(i * 4, 4), 64 * st : 64 * st + 64, :] = o.astype(BF16).reshape(4, 64, HD)
-            return carry
-
-        lax.fori_loop(0, 2, body, 0)
-
-    def attend_rest(j):
-        o = attend(Q[1024:1088, :]).reshape(SEQ, REST, HD)
-        OB[j, :, 128:144, :] = jnp.concatenate([o, jnp.zeros_like(o)], axis=1).astype(BF16)
+        weight = jnp.exp2((scores - jnp.max(scores, axis=-1, keepdims=True)) * SCALE)
+        mixed = jnp.dot(weight.astype(BF16), V[...], preferred_element_type=F32)
+        return mixed[:, :HD] / mixed[:, HD:]
+
+    def attend(j):
+        first = attend_rows(Q[0:544, :])
+        second = attend_rows(Q[544:1088, :])
+        OB[j, :, 0:64, :] = first[0:512].astype(BF16).reshape(SEQ, 64, HD)
+        image_rows = jnp.concatenate([first[512:544], second[0:480]], axis=0)
+        OB[j, :, 64:128, :] = image_rows.astype(BF16).reshape(SEQ, 64, HD)
+        rest_rows = second[480:544].reshape(SEQ, REST, HD)
+        OB[j, :, 128:144, :] = jnp.concatenate([rest_rows, jnp.zeros_like(rest_rows)], axis=1).astype(BF16)
 
     def give(j):
         lanes = pl.ds(pl.multiple_of((S * HEADS_HERE + j) * HD, HD), HD)
@@ -294,42 +271,54 @@
 
     def parts_of(j):
         return [
-            lambda: (sib_arrived(j), project(j, 0), finish(0)),
-            lambda: (project(j, 1), finish(1)),
-            lambda: attend_full(j, 0),
-            lambda: (attend_full(j, 1), attend_rest(j), give(j)),
+            lambda: (sib_arrived(j), project(j, 0)),
+            lambda: project(j, 1),
+            lambda: (attend(j), give(j)),
         ]
 
+    OWN, PARTNER = 0, 1
     begin(0)
     begin_partner(0)
-    for step in (1, 2):
-        for w in (0, 1):
-            hop(0, w, step)
+    begin(1)
+    gather_rows(2)
+    b2 = block(2, yh, z, core)
+    send(b2, b2, y_s.at[2], y_r.at[2], yp)
+    send_tokens(S, 0, d_xr)
+    send_tokens(S, 2, d_xl)
+    send_tokens(S, 4, d_yp)
+    begin_partner(1)
+    units = ((0, OWN), (0, PARTNER), (1, OWN), (1, PARTNER))
+    for j, w in units:
+        hop(j, w, 1)
+    hop(0, OWN, 2)
+    hop(0, PARTNER, 2)
     tokens_arrived(s_xl, 0, d_xr)
     send(T.at[s_xl, 0:64], T.at[s_xl, 0:64], tok_s.at[6], tok_r.at[6], d_xr)
     tokens_arrived(s_xr, 2, d_xl)
     send(T.at[s_xr, 64:128], T.at[s_xr, 64:128], tok_s.at[7], tok_r.at[7], d_xl)
     send(RM.at[s_xr], RM.at[s_xr], tok_s.at[8], tok_r.at[8], d_xl)
+    hop(1, OWN, 2)
+    hop(1, PARTNER, 2)
     tokens_arrived(s_yp, 4, d_yp)
     send_tokens(s_yp, 9, d_xr)
     send_tokens(s_yp, 11, d_xl)
-    for w in (0, 1):
-        hop(0, w, 3)
-    begin(1)
-    begin_partner(1)
-    for w in (0, 1):
-        hop(0, w, 4)
-    for w in (0, 1):
-        hop(1, w, 1)
+    hop(0, OWN, 3)
+    hop(0, PARTNER, 3)
+    b2 = block(2, yh, z, core)
+    send(b2, b2, zr_s.at[2, 0, 0], zr_r.at[2, 0, 0], zr)
+    send(b2, b2, zl_s.at[2, 0, 0], zl_r.at[2, 0, 0], zl)
+    sib_send(2, 0, 0, z)
     arrived(T.at[s_xx, 0:64], tok_s.at[6], tok_r.at[6], d_xr)
     arrived(T.at[s_xx, 64:128], tok_s.at[7], tok_r.at[7], d_xl)
     arrived(RM.at[s_xx], tok_s.at[8], tok_r.at[8], d_xl)
     send_tokens(s_xx, 13, d_yp)
-    for step in (2, 3):
-        for w in (0, 1):
-            hop(1, w, step)
-    begin(2)
+    hop(1, OWN, 3)
     begin_partner(2)
+    hop(1, PARTNER, 3)
+    for j, w in units:
+        hop(j, w, 4)
+    hop(2, OWN, 1)
+    hop(2, PARTNER, 1)
     tokens_arrived(o_xl, 9, d_xr)
     tokens_arrived(o_xr, 11, d_xl)
     tokens_arrived(o_xx, 13, d_yp)
@@ -341,13 +330,11 @@
         return carry
 
     lax.fori_loop(0, 4, unpack, 0)
-    for w in (0, 1):
-        hop(1, w, 4)
+    V[:, HD:] = jnp.ones((TOTAL, HD), BF16)
     todo = parts_of(0) + parts_of(1)
-    for step in (1, 2, 3, 4):
+    for step in (2, 3, 4):
         for w in (0, 1):
-            if todo:
-                todo.pop(0)()
+            todo.pop(0)()
             hop(2, w, step)
     for part in todo + parts_of(2):
         part()
@@ -358,8 +345,8 @@
 
 
 def on_device(text_tokens, image_tokens, weights, qk_gain, mod_table, text_lengths, time_index):
-    mods = lax.dynamic_index_in_dim(mod_table, time_index[0], 0, keepdims=False).reshape(4, D)
-    wsrc = jnp.pad(jnp.swapaxes(weights, 1, 2), ((0, 0), (0, 0), (0, 16 - WROWS), (0, 0)))
+    mods = lax.dynamic_index_in_dim(mod_table, time_index[0], 0, keepdims=False)
+    wraw = jnp.swapaxes(weights, 1, 2)
     cosine, sine = rope_rows()
     vmem = pl.BlockSpec(memory_space=pltpu.VMEM)
     dma = pltpu.SemaphoreType.DMA
@@ -370,15 +357,15 @@
         in_specs=[vmem] * 7 + [pl.BlockSpec(memory_space=pltpu.SMEM)],
         out_specs=vmem,
         scratch_shapes=[
+            pltpu.VMEM((2, 3, 16, D), BF16),
             pltpu.VMEM((HEADS_HERE, 2, 2, D // 2, 3 * HD), BF16),
             pltpu.VMEM((HEADS_HERE, 2, 3, 128, HD), BF16),
             pltpu.VMEM((SEQ, 128, D), BF16),
             pltpu.VMEM((SEQ, 16, D // 2), BF16),
             pltpu.VMEM((SEQ * REST, D), BF16),
-            pltpu.VMEM((IMG, 3 * HD), F32),
             pltpu.VMEM((TOTAL, HD), BF16),
             pltpu.VMEM((TOTAL, HD), BF16),
-            pltpu.VMEM((TOTAL, HD), BF16),
+            pltpu.VMEM((TOTAL, 2 * HD), BF16),
             pltpu.VMEM((HEADS_HERE, SEQ, 144, HD), BF16),
             pltpu.VMEM((8, TXT), F32),
             pltpu.VMEM((96, 128), BF16),
@@ -392,12 +379,12 @@
             dma((3,)),
         ],
         compiler_params=pltpu.CompilerParams(
-            collective_id=0, has_side_effects=True, vmem_limit_bytes=56 * 1024 * 1024
+            collective_id=0, has_side_effects=True, vmem_limit_bytes=36 * 1024 * 1024
         ),
         cost_estimate=pl.CostEstimate(flops=9_500_000_000, bytes_accessed=30_000_000, transcendentals=3_600_000),
         name="joint_attention",
     )(
-        wsrc, text_tokens[0], image_tokens[0], mods, qk_gain.reshape(4, HD),
+        wraw, text_tokens[0], image_tokens[0], mods, qk_gain.reshape(4, HD),
         jnp.asarray(cosine), jnp.asarray(sine), text_lengths.astype(jnp.int32),
     )
     return result[None, :TROWS], result[None, TROWS : TROWS + IROWS]

time: 146 us -> 118 us (0.81)
  Pallas kernels: 138 us -> 108 us
    pallas_call x1, Pallas kernels: 138 us -> 108 us  [on_device(): pl.pallas_call(kernel, out_shape=jax.ShapeDtypeStruct((144, D), BF16), in...]
    unnamed x3 -> x13, local copies, waits for them, and re-layouts: 1.11 us -> 5.72 us
    broadcast_in_dim x2, local copies, waits for them, and re-layouts: 3.57 us -> 1.57 us  [on_device(): return (result[None, :TROWS], result[None, TROWS:TROWS + IROWS])]
where the time goes in v2:
time: 118 us
  Pallas kernels  108 us (92%)
  local copies, waits for them, and re-layouts  7.3 us (6%)
  between operations  2.09 us (2%)
    pallas_call x1, Pallas kernels, on_device(): pl.pallas_call(kernel, out_shape=jax.ShapeDtypeStruct((144, D), BF16), in...  108 us
    unnamed x13, local copies, waits for them, and re-layouts  5.72 us

profile of v2, /device:TPU:1, one launch (start us, length us, event | category | flops | bytes accessed | tf_op | source)
XLA Modules:
  0.0 117.7 jit_solution(10682492280337608563)
XLA Ops:
  0.6 0.0 copy-start
  2.0 0.0 copy-done
  2.1 1.1 copy.13
  3.2 0.0 copy-start.1
  3.2 1.0 copy-done.1
  4.2 0.0 copy-start.2
  4.2 1.0 copy-done.2
  5.2 0.0 copy-start.3
  5.2 0.7 copy-done.3
  5.9 0.0 copy-start.4
  5.9 1.0 copy-done.4
  6.8 0.0 copy-start.5
  6.8 1.0 copy-done.5
  7.8 108.3 %joint_attention.1 = bf16[144,3072]{1,0:T(8,128)(2,1)S(1)} custom-call(bf16[2,3,12,3072]{3,2,1,0:T(8,128)(2,1)S(1)} %bitcast.16, bf16[64,3072]{1,0:T(8,128)(2,1)S(1)} %bitcast.18, bf16[72,3072]{1,0:T(8,128)(2,1)S(1)} %bitcast.17, f32[2,2,3072]{2,1,0:T(2,128)S(1)} %dynamic-slice_bitcast_fusion.mods, f32[4,128]{1,0:T(4,128)S(1)} %bitcast.19, ...), custom_call_target="tpu_custom_call" | custom-call | flops 9500000256 | bytes 30000000 | tf_op jit(solution)/shard_map/joint_attention/pallas_call | solution.py:354
  116.1 0.8 slice_bitcast_fusion.1
  116.9 0.8 slice_bitcast_fusion
  (1 shorter events, 0.0 us)
Async XLA Ops:
  0.6 1.4 %copy-start = (f32[28,2,2,3072]{3,2,1,0:T(2,128)S(1)}, f32[28,2,2,3072]{3,2,1,0:T(2,128)}, u32[]{:S(2)}) copy-start(f32[28,2,2,3072]{3,2,1,0:T(2,128)} %param.13) | copy-start | bytes 4128772
  3.2 1.0 copy-start.1
  4.2 1.0 copy-start.2
  5.2 0.7 copy-start.3
  5.9 1.0 copy-start.4
  6.8 1.0 copy-start.5

commit v3 on v2

v3 whole, which is shorter than its diff:
```python
import functools

import jax
import jax.numpy as jnp
import numpy as np
from jax import lax
from jax.experimental import pallas as pl
from jax.experimental.pallas import tpu as pltpu
from jax.sharding import PartitionSpec as P

D = 3072
HD = 128
GRID = 24
TXT = 512
IMG = GRID * GRID
TOTAL = TXT + IMG
SEQ = 8
NZ = 8
HEADS_HERE = 3
TROWS = TXT // SEQ
IROWS = IMG // SEQ
REST = IROWS - 64
WROWS = 12
KSTEP = 768
SCALE = float(HD**-0.5 * np.log2(np.e))
MESH = pl.DeviceIdType.MESH
BF16, F32 = jnp.bfloat16, jnp.float32


def rope_rows():
    pairs, still = HD // 2, HD // 16
    rows = (pairs - still) // 2
    cols = pairs - still - rows
    place = np.concatenate(
        [
            (np.arange(SEQ)[:, None] * IROWS + np.arange(64)[None, :]).reshape(-1),
            (np.arange(SEQ)[:, None] * IROWS + 64 + np.arange(REST)[None, :]).reshape(-1),
        ]
    )
    row_pos = (place // GRID).astype(np.float32)
    col_pos = (place % GRID).astype(np.float32)
    row_freq = (10000.0 ** (-np.arange(rows) / rows)).astype(np.float32)
    col_freq = (10000.0 ** (-np.arange(cols) / cols)).astype(np.float32)
    angles = np.concatenate(
        [
            np.zeros((IMG, still), np.float32),
            row_pos[:, None] * row_freq[None, :],
            col_pos[:, None] * col_freq[None, :],
        ],
        axis=1,
    )
    cosine = np.repeat(np.cos(angles), 2, axis=1)
    sine = np.repeat(np.sin(angles), 2, axis=1)
    sine[:, 0::2] *= -1.0
    return cosine.astype(np.float32), sine.astype(np.float32)


def kernel(
    wraw, text_hbm, image_hbm, mods_hbm, gains_hbm, cosine_hbm, sine_hbm, length, step_index,
    out,
    picked,     text, image, mods, gains, cosine, sine, wsrc, W, A, T, RM, XR, Q, K, V, OB, bias, sel, acc,
    a2a_s, a2a_r, y_s, y_r, zr_s, zr_r, zl_s, zl_r, sib_s, sib_r, yc_s, yc_r, sc_s, sc_r, tok_s, tok_r, out_s, out_r, own_sem, load_sem,
):
    R, S = lax.axis_index("rep"), lax.axis_index("seq")
    core = lax.rem(R, 2)
    z = lax.rem(R // 2, NZ)
    yh = R // (2 * NZ)
    x = lax.rem(S, 4)
    yl = S // 4

    def rep_of(y, zz, c):
        return (y * NZ + zz) * 2 + c

    def up(dz):
        return lax.rem(z + dz + NZ, NZ)

    def xs(dx, row):
        return row * 4 + lax.rem(x + dx + 4, 4)

    sib = (rep_of(yh, z, 1 - core), S)
    zr = (rep_of(yh, up(1), core), S)
    zl = (rep_of(yh, up(-1), core), S)
    yp = (rep_of(1 - yh, z, core), S)
    peers = [(R, lax.rem(S + d, SEQ)) for d in range(1, SEQ)]
    s_yp, s_xr, s_xl, s_xx = xs(0, 1 - yl), xs(1, yl), xs(-1, yl), xs(2, yl)
    o_xr, o_xl, o_xx = xs(1, 1 - yl), xs(-1, 1 - yl), xs(2, 1 - yl)

    loads = []
    for i, (far, near) in enumerate(
        [(mods_hbm, mods), (text_hbm, text), (image_hbm, image), (gains_hbm, gains), (cosine_hbm, cosine), (sine_hbm, sine)]
    ):
        loads.append(pltpu.make_async_copy(far, near, load_sem.at[i]))
        loads[-1].start()

    wsrc[:, :, 0:WROWS, :] = wraw[...]
    wsrc[:, :, WROWS:16, :] = jnp.zeros((2, 3, 16 - WROWS, D), BF16)

    barrier = pltpu.get_barrier_semaphore()
    partners = [sib, zr, zl, yp] + peers
    for device in partners:
        pl.semaphore_signal(barrier, inc=1, device_id=device, device_id_type=MESH)
    pl.semaphore_wait(barrier, len(partners))

    pending = []

    def send(src, dst, ssem, rsem, device):
        copy = pltpu.make_async_remote_copy(
            src_ref=src, dst_ref=dst, send_sem=ssem, recv_sem=rsem, device_id=device, device_id_type=MESH
        )
        copy.start()
        pending.append(copy)

    def arrived(dst, ssem, rsem, device):
        pltpu.make_async_remote_copy(
            src_ref=dst, dst_ref=dst, send_sem=ssem, recv_sem=rsem, device_id=device, device_id_type=MESH
        ).wait_recv()

    def slot(j, s):
        return A.at[j, :, :, pl.ds(pl.multiple_of(s * 16, 16), 16), :]

    def piece(j, g):
        return wsrc.at[:, :, :, pl.ds(pl.multiple_of(g * (HEADS_HERE * HD) + j * HD, HD), HD)]

    def a2a_start(j):
        for d in range(1, SEQ):
            send(piece(j, peers[d - 1][1]), slot(j, S), a2a_s.at[j, d - 1], a2a_r.at[j, d - 1], peers[d - 1])
        copy = pltpu.make_async_copy(piece(j, S), slot(j, S), own_sem.at[j])
        copy.start()
        return copy

    own_copies = [a2a_start(0)]

    i96 = lax.broadcasted_iota(jnp.int32, (96, 128), 0)
    i128 = lax.broadcasted_iota(jnp.int32, (96, 128), 1)
    sel[...] = jnp.where(i128 == (i96 // WROWS) * 16 + lax.rem(i96, WROWS), 1.0, 0.0).astype(BF16)

    for copy in loads[:3]:
        copy.wait()
    for stream in range(2):
        row = jnp.zeros((2, D), F32)
        for i in range(mods.shape[0]):
            row = row + jnp.where(step_index[...] == i, mods[i, stream], 0.0)
        picked[stream] = row

    def modulate(rows, stream):
        v = rows.astype(F32)
        center = v - jnp.mean(v, axis=-1, keepdims=True)
        spread = jnp.mean(center * center, axis=-1, keepdims=True)
        normed = center * lax.rsqrt(spread + 1e-06)
        return normed * (1.0 + picked[stream, 1:2, :]) + picked[stream, 0:1, :]

    def mod_text(i, carry):
        rows = pl.ds(pl.multiple_of(i * 16, 16), 16)
        T[S, rows, :] = modulate(text[rows, :], 0).astype(BF16)
        return carry

    def mod_image(i, carry):
        rows = pl.ds(pl.multiple_of(i * 16, 16), 16)
        T[S, pl.ds(pl.multiple_of(64 + i * 16, 16), 16), :] = modulate(image[rows, :], 1).astype(BF16)
        return carry

    lax.fori_loop(0, 4, mod_text, 0)
    lax.fori_loop(0, 4, mod_image, 0)
    rest = modulate(image[64:72, :], 1)
    RM[S] = jnp.concatenate([rest[:, : D // 2], rest[:, D // 2 :]], axis=0).astype(BF16)

    def send_tokens(s, first, device):
        send(T.at[s], T.at[s], tok_s.at[first], tok_r.at[first], device)
        send(RM.at[s], RM.at[s], tok_s.at[first + 1], tok_r.at[first + 1], device)

    def tokens_arrived(s, first, device):
        arrived(T.at[s], tok_s.at[first], tok_r.at[first], device)
        arrived(RM.at[s], tok_s.at[first + 1], tok_r.at[first + 1], device)

    own_copies.append(a2a_start(1))
    d_yp, d_xr, d_xl = (R, s_yp), (R, s_xr), (R, s_xl)
    def rows_of(zz, c):
        return pl.ds(pl.multiple_of((zz * 2 + c) * 96, 32), 96)

    def block(j, y, zz, c):
        return W.at[j, :, y, rows_of(zz, c), :]

    def half(j, st, y, zz, c):
        return W.at[j, st, y, rows_of(zz, c), :]

    def gather_rows(j):
        own_copies[j].wait()
        for d in range(1, SEQ):
            src = lax.rem(S + SEQ - d, SEQ)
            arrived(slot(j, src), a2a_s.at[j, d - 1], a2a_r.at[j, d - 1], peers[d - 1])
        for st in range(2):
            rows = jnp.concatenate([A[j, st, q] for q in range(3)], axis=1)
            W[j, st, yh, rows_of(z, core), :] = jnp.dot(sel[...], rows, preferred_element_type=F32).astype(BF16)

    yy = [yh, 1 - yh]

    def split(j, w):
        return (j, w) == (2, 1)

    def ring_block(j, w, zz):
        return half(j, 0, yy[w], zz, core) if split(j, w) else block(j, yy[w], zz, core)

    def sib_send(j, w, k, zz):
        b = ring_block(j, w, zz) if k else block(j, yy[w], zz, core)
        send(b, b, sib_s.at[j, w, k], sib_r.at[j, w, k], sib)

    def first(j, w):
        b = ring_block(j, w, z)
        send(b, b, zr_s.at[j, w, 0], zr_r.at[j, w, 0], zr)
        send(b, b, zl_s.at[j, w, 0], zl_r.at[j, w, 0], zl)
        sib_send(j, w, 0, z)

    def collect(j):
        gather_rows(j)
        b = block(j, yh, z, core)
        send(b, b, y_s.at[j], y_r.at[j], yp)

    def partner_rows(j):
        arrived(block(j, 1 - yh, z, core), y_s.at[j], y_r.at[j], yp)

    def cross(j, w, k, zz):
        if split(j, 1) and w == 0:
            b = half(j, 1, yh, zz, core)
            send(b, b, yc_s.at[k - 1], yc_r.at[k - 1], yp)

    def cross_arrived(j, ks):
        if not split(j, 1):
            return
        for k, dz in ((1, -1), (2, -2), (3, -3), (4, 1), (5, 2), (6, 3), (7, 4)):
            if k not in ks:
                continue
            b = half(j, 1, 1 - yh, up(dz), core)
            arrived(b, yc_s.at[k - 1], yc_r.at[k - 1], yp)
            send(b, b, sc_s.at[k - 1], sc_r.at[k - 1], sib)

    def hop(j, w, step):
        if step < 4:
            for sems, sign, k in (((zr_s, zr_r, zr), -1, step), ((zl_s, zl_r, zl), 1, step + 3)):
                b = ring_block(j, w, up(sign * step))
                arrived(b, sems[0].at[j, w, step - 1], sems[1].at[j, w, step - 1], sems[2])
                f = b if step < 3 else half(j, 0 if sign < 0 else 1, yy[w], up(sign * step), core)
                if step < 3 or sign < 0 or not split(j, w):
                    send(f, f, sems[0].at[j, w, step], sems[1].at[j, w, step], sems[2])
                sib_send(j, w, k, up(sign * step))
                cross(j, w, k, up(sign * step))
        else:
            arrived(half(j, 0, yy[w], up(4), core), zr_s.at[j, w, 3], zr_r.at[j, w, 3], zr)
            if not split(j, w):
                arrived(half(j, 1, yy[w], up(4), core), zl_s.at[j, w, 3], zl_r.at[j, w, 3], zl)
            sib_send(j, w, 7, up(4))
            cross(j, w, 7, up(4))

    def sib_arrived(j, ks=range(8)):
        for w in range(2):
            for k, dz in enumerate((0, -1, -2, -3, 1, 2, 3, 4)):
                if k not in ks:
                    continue
                whole = block(j, yy[w], up(dz), 1 - core)
                b = half(j, 0, yy[w], up(dz), 1 - core) if k and split(j, w) else whole
                arrived(b, sib_s.at[j, w, k], sib_r.at[j, w, k], sib)
                if k and split(j, w):
                    b = half(j, 1, yy[w], up(dz), 1 - core)
                    arrived(b, sc_s.at[k - 1], sc_r.at[k - 1], sib)

    def prepare(j, st, rows, places, start):
        def table(ref):
            return jnp.concatenate([ref[pl.ds(at - start, n), :] for at, n in places], axis=0)

        for part, store in ((0, Q), (1, K), (2, V)):
            v = rows[:, part * HD : (part + 1) * HD]
            if part < 2:
                power = jnp.mean(v * v, axis=-1, keepdims=True)
                v = v * lax.rsqrt(power + 1e-06) * gains[2 * st + part : 2 * st + part + 1, :]
                if st == 1:
                    even = lax.rem(lax.broadcasted_iota(jnp.int32, v.shape, 1), 2) == 0
                    turned = jnp.where(even, pltpu.roll(v, HD - 1, 1), pltpu.roll(v, 1, 1))
                    v = v * table(cosine) + turned * table(sine)
            v = v.astype(BF16)
            done = 0
            for at, n in places:
                store[j, pl.ds(at, n), 0:HD] = v[done : done + n]
                done += n

    near, distant = (S, s_xl, s_xr, s_yp, s_xx), (o_xl, o_xr, o_xx)

    def project(j, st, slots):
        base = TXT * st
        lhs = [T[s, 64 * st : 64 * st + 64, :] for s in slots]
        places = [(pl.multiple_of(base + s * 64, 64), 64) for s in slots]
        if st == 1 and slots is distant:
            lhs.append(XR[...])
            places.append((TXT + 512, 64))
        rows = jnp.dot(
            jnp.concatenate(lhs, axis=0), W[j, st].reshape(D, 3 * HD), preferred_element_type=F32
        )
        prepare(j, st, rows, places, TXT)

    def partial(j, st, quarters):
        total = None
        for q in quarters:
            cols = [pl.ds(pl.multiple_of(y * (D // 2) + q * 384, 128), 384) for y in range(2)]
            lhs = jnp.concatenate(
                [T[:, 64 * st : 64 * st + 64, c].reshape(SEQ * 64, 384) for c in cols], axis=1
            )
            if st == 1:
                lhs = jnp.concatenate([lhs, jnp.concatenate([XR[:, c] for c in cols], axis=1)], axis=0)
            rhs = jnp.concatenate([W[j, st, y, pl.ds(pl.multiple_of(q * 384, 128), 384), :] for y in range(2)], axis=0)
            term = jnp.dot(lhs, rhs, preferred_element_type=F32)
            total = term if total is None else total + term
        return total

    quarter = z // 2

    def project_some(j, st, quarters):
        at, n = ((0, TXT), (TXT, IMG))[st]
        total = partial(j, st, quarters)
        acc[at : at + n, :] = total if len(quarters) == 2 else acc[at : at + n, :] + total

    side = 2 * lax.rem(z, 2) - 1
    order = [quarter, lax.rem(quarter + side + 4, 4), lax.rem(quarter - side + 4, 4), lax.rem(quarter + 2, 4)]

    def project_last(j):
        for st, at, n in ((0, 0, TXT), (1, TXT, IMG)):
            rows = acc[at : at + n, :] + partial(j, st, order[3:])
            prepare(j, st, rows, [(at, n)], TXT)

    def attend_rows(j, q):
        scores = lax.dot_general(q, K[j], (((1,), (1,)), ((), ())), preferred_element_type=F32)
        scores = jnp.concatenate([scores[:, :TXT] + bias[0:1, :], scores[:, TXT:]], axis=1)
        weight = jnp.exp2((scores - jnp.max(scores, axis=-1, keepdims=True)) * SCALE)
        mixed = jnp.dot(weight.astype(BF16), V[j], preferred_element_type=F32)
        return mixed[:, :HD] / mixed[:, HD:]

    def attend(j):
        first = attend_rows(j, Q[j, 0:544, :])
        second = attend_rows(j, Q[j, 544:1088, :])
        OB[j, :, 0:64, :] = first[0:512].astype(BF16).reshape(SEQ, 64, HD)
        image_rows = jnp.concatenate([first[512:544], second[0:480]], axis=0)
        OB[j, :, 64:128, :] = image_rows.astype(BF16).reshape(SEQ, 64, HD)
        rest_rows = second[480:544].reshape(SEQ, REST, HD)
        OB[j, :, 128:144, :] = jnp.concatenate([rest_rows, jnp.zeros_like(rest_rows)], axis=1).astype(BF16)

    def give(j):
        lanes = pl.ds(pl.multiple_of((S * HEADS_HERE + j) * HD, HD), HD)
        for d in range(1, SEQ):
            send(OB.at[j, peers[d - 1][1]], out.at[:, lanes], out_s.at[j, d - 1], out_r.at[j, d - 1], peers[d - 1])
        out[:, lanes] = OB[j, S]

    def take(j):
        for d in range(1, SEQ):
            src = lax.rem(S + SEQ - d, SEQ)
            lanes = pl.ds(pl.multiple_of((src * HEADS_HERE + j) * HD, HD), HD)
            arrived(out.at[:, lanes], out_s.at[j, d - 1], out_r.at[j, d - 1], peers[d - 1])

    def unpack(i, carry):
        pair = [RM[2 * i + n].astype(F32) for n in range(2)]
        rows = [jnp.concatenate([p[0:8], p[8:16]], axis=1) for p in pair]
        XR[pl.ds(pl.multiple_of(i * 16, 16), 16), :] = jnp.concatenate(rows, axis=0).astype(BF16)
        return carry

    def text_half(s):
        return T.at[s, 0:64]

    def image_half(s):
        return T.at[s, 64:128]

    def pass_on(parts, start, device):
        for i, part in enumerate(parts):
            send(part, part, tok_s.at[start + i], tok_r.at[start + i], device)

    def came(parts, start, device):
        for i, part in enumerate(parts):
            arrived(part, tok_s.at[start + i], tok_r.at[start + i], device)

    def near_came():
        tokens_arrived(s_xl, 0, d_xr)
        pass_on([text_half(s_xl)], 6, d_xr)
        tokens_arrived(s_xr, 2, d_xl)
        pass_on([image_half(s_xr), RM.at[s_xr]], 7, d_xl)

    def partner_came():
        tokens_arrived(s_yp, 4, d_yp)
        pass_on([T.at[s_yp], RM.at[s_yp]], 9, d_xr)
        pass_on([T.at[s_yp], RM.at[s_yp]], 11, d_xl)

    def opposite_came():
        came([text_half(s_xx)], 6, d_xr)
        came([image_half(s_xx), RM.at[s_xx]], 7, d_xl)
        pass_on([T.at[s_xx], RM.at[s_xx]], 13, d_yp)

    def all_came():
        tokens_arrived(o_xl, 9, d_xr)
        tokens_arrived(o_xr, 11, d_xl)
        tokens_arrived(o_xx, 13, d_yp)
        lax.fori_loop(0, 4, unpack, 0)

    OWN, PARTNER = 0, 1

    def hops(j, step):
        hop(j, OWN, step)
        hop(j, PARTNER, step)

    collect(0)
    first(0, OWN)
    where = lax.broadcasted_iota(jnp.int32, (8, TXT), 1)
    bias[...] = jnp.where(where < length[...], 0.0, -jnp.inf).astype(F32)
    collect(1)
    first(1, OWN)
    send_tokens(S, 0, d_xr)
    send_tokens(S, 2, d_xl)
    partner_rows(0)
    first(0, PARTNER)
    partner_rows(1)
    first(1, PARTNER)
    send_tokens(S, 4, d_yp)
    own_copies.append(a2a_start(2))
    V[:, :, HD:] = jnp.ones((HEADS_HERE, TOTAL, HD), BF16)
    hops(0, 1)
    hops(1, 1)
    hops(0, 2)
    near_came()
    hops(1, 2)
    collect(2)
    partner_came()
    hops(0, 3)
    first(2, OWN)
    opposite_came()
    hop(1, OWN, 3)
    partner_rows(2)
    first(2, PARTNER)
    hop(1, PARTNER, 3)
    hops(0, 4)
    hop(2, OWN, 1)
    hop(1, OWN, 4)
    hop(2, PARTNER, 1)
    hop(1, PARTNER, 4)
    for copy in loads[3:]:
        copy.wait()
    sib_arrived(0)
    project(0, 0, near)
    project(0, 1, near)
    sib_arrived(1)
    project(1, 0, near)
    project(1, 1, near)
    hop(2, OWN, 2)
    all_came()
    project(0, 0, distant)
    hop(2, PARTNER, 2)
    project(0, 1, distant)
    attend(0)
    hop(2, OWN, 3)
    give(0)
    hop(2, PARTNER, 3)
    project(1, 0, distant)
    project(1, 1, distant)
    cross_arrived(2, (1, 2, 4, 5))
    sib_arrived(2, (0, 1, 2, 4, 5))
    project_some(2, 0, order[0:2])
    hop(2, OWN, 4)
    hop(2, PARTNER, 4)
    project_some(2, 1, order[0:2])
    attend(1)
    give(1)
    cross_arrived(2, (3, 6, 7))
    sib_arrived(2, (3, 6))
    project_some(2, 0, order[2:3])
    project_some(2, 1, order[2:3])
    sib_arrived(2, (7,))
    project_last(2)
    attend(2)
    give(2)
    for j in range(HEADS_HERE):
        take(j)
    for copy in pending:
        copy.wait_send()


def cut(rows, text, image):
    text[0] = rows[0:TROWS, :]
    image[0] = rows[TROWS : TROWS + IROWS, :]


def on_device(text_tokens, image_tokens, weights, qk_gain, mod_table, text_lengths, time_index):
    wraw = jnp.swapaxes(weights, 1, 2)
    cosine, sine = rope_rows()
    vmem = pl.BlockSpec(memory_space=pltpu.VMEM)
    dma = pltpu.SemaphoreType.DMA
    n_tok = 15
    result = pl.pallas_call(
        kernel,
        out_shape=jax.ShapeDtypeStruct((144, D), BF16),
        in_specs=[vmem] + [pl.BlockSpec(memory_space=pltpu.HBM)] * 6 + [vmem] * 2,
        out_specs=vmem,
        scratch_shapes=[
            pltpu.VMEM((2, 2, D), F32),
            pltpu.VMEM(text_tokens.shape[1:], BF16),
            pltpu.VMEM(image_tokens.shape[1:], BF16),
            pltpu.VMEM(mod_table.shape, F32),
            pltpu.VMEM((4, HD), F32),
            pltpu.VMEM((IMG, HD), F32),
            pltpu.VMEM((IMG, HD), F32),
            pltpu.VMEM((2, 3, 16, D), BF16),
            pltpu.VMEM((HEADS_HERE, 2, 2, D // 2, 3 * HD), BF16),
            pltpu.VMEM((HEADS_HERE, 2, 3, 128, HD), BF16),
            pltpu.VMEM((SEQ, 128, D), BF16),
            pltpu.VMEM((SEQ, 16, D // 2), BF16),
            pltpu.VMEM((SEQ * REST, D), BF16),
            pltpu.VMEM((HEADS_HERE, TOTAL, HD), BF16),
            pltpu.VMEM((HEADS_HERE, TOTAL, HD), BF16),
            pltpu.VMEM((HEADS_HERE, TOTAL, 2 * HD), BF16),
            pltpu.VMEM((HEADS_HERE, SEQ, 144, HD), BF16),
            pltpu.VMEM((8, TXT), F32),
            pltpu.VMEM((96, 128), BF16),
            pltpu.VMEM((TOTAL, 3 * HD), F32),
            dma((3, 7)), dma((3, 7)),
            dma((3,)), dma((3,)),
            dma((3, 2, 4)), dma((3, 2, 4)),
            dma((3, 2, 4)), dma((3, 2, 4)),
            dma((3, 2, 8)), dma((3, 2, 8)),
            dma((7,)), dma((7,)),
            dma((7,)), dma((7,)),
            dma((n_tok,)), dma((n_tok,)),
            dma((3, 7)), dma((3, 7)),
            dma((3,)),
            dma((6,)),
        ],
        compiler_params=pltpu.CompilerParams(
            collective_id=0, has_side_effects=True, vmem_limit_bytes=56 * 1024 * 1024
        ),
        cost_estimate=pl.CostEstimate(flops=9_500_000_000, bytes_accessed=30_000_000, transcendentals=3_600_000),
        name="joint_attention",
    )(
        wraw, text_tokens[0], image_tokens[0], mod_table, qk_gain.reshape(4, HD),
        jnp.asarray(cosine), jnp.asarray(sine), text_lengths.astype(jnp.int32).reshape(1, 1),
        time_index.astype(jnp.int32).reshape(1, 1),
    )
    return pl.pallas_call(
        cut,
        out_shape=(
            jax.ShapeDtypeStruct((1, TROWS, D), BF16),
            jax.ShapeDtypeStruct((1, IROWS, D), BF16),
        ),
        in_specs=[vmem],
        out_specs=(vmem, vmem),
        name="cut_outputs",
    )(result)


def solution(mesh):
    placed = (
        P("rep", "seq", None),
        P("rep", "seq", None),
        P(None, ("rep", "seq"), None, None),
        P(),
        P(),
        P("rep"),
        P("rep"),
    )
    return jax.shard_map(
        on_device,
        mesh=mesh,
        in_specs=placed,
        out_specs=(P("rep", "seq", None), P("rep", "seq", None)),
        check_vma=False,
    )
```

time: 118 us -> 107 us (0.907)
  local copies, waits for them, and re-layouts: 7.3 us -> 1.93 us
  Pallas kernels: 108 us -> 103 us
    pallas_call x1, Pallas kernels: 108 us -> 101 us  [on_device(): pl.pallas_call(kernel, out_shape=jax.ShapeDtypeStruct((144, D), BF16), in...]
    unnamed x13 -> x1, local copies, waits for them, and re-layouts: 5.72 us -> 1.93 us
    pallas_call x0 -> x1, Pallas kernels: none -> 2.09 us  [on_device(): pl.pallas_call(cut, out_shape=(jax.ShapeDtypeStruct((1, TROWS, D), BF16),...]
    broadcast_in_dim x2 -> x0, local copies, waits for them, and re-layouts: 1.57 us -> none  [on_device(): return (result[None, :TROWS], result[None, TROWS:TROWS + IROWS])]
where the time goes in v3:
time: 107 us
  Pallas kernels  103 us (96%)
  local copies, waits for them, and re-layouts  1.93 us (2%)
  between operations  1.93 us (2%)
    pallas_call x1, Pallas kernels, on_device(): pl.pallas_call(kernel, out_shape=jax.ShapeDtypeStruct((144, D), BF16), in...  101 us

profile of v3, /device:TPU:1, one launch (start us, length us, event | category | flops | bytes accessed | tf_op | source)
XLA Modules:
  0.0 106.8 jit_solution(12912682628067899742)
XLA Ops:
  1.9 1.9 %copy.13 = bf16[2,12,3,3072]{3,1,2,0:T(8,128)(2,1)} copy(bf16[2,12,3,3072]{3,0,2,1:T(2,128)(2,1)} %param.11) | data formatting | bytes 884736 | tf_op args[2]
  3.9 100.8 %joint_attention.1.rows = bf16[144,3072]{1,0:T(8,128)(2,1)} custom-call(bf16[2,3,12,3072]{3,2,1,0:T(8,128)(2,1)} %bitcast.10, bf16[64,3072]{1,0:T(8,128)(2,1)} %bitcast.12, bf16[72,3072]{1,0:T(8,128)(2,1)} %bitcast.11, f32[28,2,2,3072]{3,2,1,0:T(2,128)} %mods_hbm.1, f32[4,128]{1,0:T(4,128)} %bitcast.13, f32[576,128]{1,0:T(8,128)} %constant.4.clone.cosine_hbm, ...), custom_call_target="tpu_custom_call" | custom-call | flops 9500000256 | bytes 30000000 | tf_op jit(solution)/shard_map/joint_attention/pallas_call | solution.py:489
  104.7 2.1 %cut_outputs.1 = (bf16[1,64,3072]{2,1,0:T(8,128)(2,1)}, bf16[1,72,3072]{2,1,0:T(8,128)(2,1)}) custom-call(bf16[144,3072]{1,0:T(8,128)(2,1)} %joint_attention.1.rows), custom_call_target="tpu_custom_call" | custom-call | tf_op jit(solution)/shard_map/cut_outputs/pallas_call | solution.py:537

commit v4 on v3

--- a/solution.py
+++ b/solution.py
@@ -56,9 +56,9 @@
 
 
 def kernel(
-    wraw, text_hbm, image_hbm, mods_hbm, gains_hbm, cosine_hbm, sine_hbm, length, step_index,
+    wraw_hbm, text_hbm, image_hbm, mods_hbm, gains_hbm, cosine_hbm, sine_hbm, length, step_index,
     out,
-    picked,     text, image, mods, gains, cosine, sine, wsrc, W, A, T, RM, XR, Q, K, V, OB, bias, sel, acc,
+    wraw, picked, text, image, mods, gains, cosine, sine, wsrc, W, A, T, RM, XR, Q, K, V, OB, bias, sel, acc,
     a2a_s, a2a_r, y_s, y_r, zr_s, zr_r, zl_s, zl_r, sib_s, sib_r, yc_s, yc_r, sc_s, sc_r, tok_s, tok_r, out_s, out_r, own_sem, load_sem,
 ):
     R, S = lax.axis_index("rep"), lax.axis_index("seq")
@@ -85,20 +85,24 @@
     s_yp, s_xr, s_xl, s_xx = xs(0, 1 - yl), xs(1, yl), xs(-1, yl), xs(2, yl)
     o_xr, o_xl, o_xx = xs(1, 1 - yl), xs(-1, 1 - yl), xs(2, 1 - yl)
 
-    loads = []
-    for i, (far, near) in enumerate(
-        [(mods_hbm, mods), (text_hbm, text), (image_hbm, image), (gains_hbm, gains), (cosine_hbm, cosine), (sine_hbm, sine)]
-    ):
-        loads.append(pltpu.make_async_copy(far, near, load_sem.at[i]))
-        loads[-1].start()
-
-    wsrc[:, :, 0:WROWS, :] = wraw[...]
-    wsrc[:, :, WROWS:16, :] = jnp.zeros((2, 3, 16 - WROWS, D), BF16)
-
     barrier = pltpu.get_barrier_semaphore()
     partners = [sib, zr, zl, yp] + peers
     for device in partners:
         pl.semaphore_signal(barrier, inc=1, device_id=device, device_id_type=MESH)
+    loads = []
+    for i, (far, near) in enumerate(
+        [(wraw_hbm, wraw), (mods_hbm, mods), (text_hbm, text), (image_hbm, image), (gains_hbm, gains), (cosine_hbm, cosine), (sine_hbm, sine)]
+    ):
+        loads.append(pltpu.make_async_copy(far, near, load_sem.at[i]))
+        loads[-1].start()
+
+    loads[0].wait()
+    for q in range(3):
+        rows = wraw[:, q].astype(F32)
+        for st in range(2):
+            wsrc[st, q, 0:WROWS, :] = rows[:, st, :].astype(BF16)
+    wsrc[:, :, WROWS:16, :] = jnp.zeros((2, 3, 16 - WROWS, D), BF16)
+
     pl.semaphore_wait(barrier, len(partners))
 
     pending = []
@@ -110,6 +114,10 @@
         copy.start()
         pending.append(copy)
 
+    def flush(keep):
+        while len(pending) > keep:
+            pending.pop(0).wait_send()
+
     def arrived(dst, ssem, rsem, device):
         pltpu.make_async_remote_copy(
             src_ref=dst, dst_ref=dst, send_sem=ssem, recv_sem=rsem, device_id=device, device_id_type=MESH
@@ -128,19 +136,11 @@
         copy.start()
         return copy
 
-    own_copies = [a2a_start(0)]
+    own_copies = [a2a_start(0), a2a_start(1)]
 
     i96 = lax.broadcasted_iota(jnp.int32, (96, 128), 0)
     i128 = lax.broadcasted_iota(jnp.int32, (96, 128), 1)
     sel[...] = jnp.where(i128 == (i96 // WROWS) * 16 + lax.rem(i96, WROWS), 1.0, 0.0).astype(BF16)
-
-    for copy in loads[:3]:
-        copy.wait()
-    for stream in range(2):
-        row = jnp.zeros((2, D), F32)
-        for i in range(mods.shape[0]):
-            row = row + jnp.where(step_index[...] == i, mods[i, stream], 0.0)
-        picked[stream] = row
 
     def modulate(rows, stream):
         v = rows.astype(F32)
@@ -159,11 +159,6 @@
         T[S, pl.ds(pl.multiple_of(64 + i * 16, 16), 16), :] = modulate(image[rows, :], 1).astype(BF16)
         return carry
 
-    lax.fori_loop(0, 4, mod_text, 0)
-    lax.fori_loop(0, 4, mod_image, 0)
-    rest = modulate(image[64:72, :], 1)
-    RM[S] = jnp.concatenate([rest[:, : D // 2], rest[:, D // 2 :]], axis=0).astype(BF16)
-
     def send_tokens(s, first, device):
         send(T.at[s], T.at[s], tok_s.at[first], tok_r.at[first], device)
         send(RM.at[s], RM.at[s], tok_s.at[first + 1], tok_r.at[first + 1], device)
@@ -172,7 +167,6 @@
         arrived(T.at[s], tok_s.at[first], tok_r.at[first], device)
         arrived(RM.at[s], tok_s.at[first + 1], tok_r.at[first + 1], device)
 
-    own_copies.append(a2a_start(1))
     d_yp, d_xr, d_xl = (R, s_yp), (R, s_xr), (R, s_xl)
     def rows_of(zz, c):
         return pl.ds(pl.multiple_of((zz * 2 + c) * 96, 32), 96)
@@ -402,6 +396,17 @@
 
     collect(0)
     first(0, OWN)
+    for copy in loads[1:4]:
+        copy.wait()
+    for stream in range(2):
+        row = jnp.zeros((2, D), F32)
+        for i in range(mods.shape[0]):
+            row = row + jnp.where(step_index[...] == i, mods[i, stream], 0.0)
+        picked[stream] = row
+    lax.fori_loop(0, 4, mod_text, 0)
+    lax.fori_loop(0, 4, mod_image, 0)
+    rest = modulate(image[64:72, :], 1)
+    RM[S] = jnp.concatenate([rest[:, : D // 2], rest[:, D // 2 :]], axis=0).astype(BF16)
     where = lax.broadcasted_iota(jnp.int32, (8, TXT), 1)
     bias[...] = jnp.where(where < length[...], 0.0, -jnp.inf).astype(F32)
     collect(1)
@@ -417,11 +422,13 @@
     V[:, :, HD:] = jnp.ones((HEADS_HERE, TOTAL, HD), BF16)
     hops(0, 1)
     hops(1, 1)
+    flush(48)
     hops(0, 2)
     near_came()
     hops(1, 2)
     collect(2)
     partner_came()
+    flush(48)
     hops(0, 3)
     first(2, OWN)
     opposite_came()
@@ -430,15 +437,16 @@
     first(2, PARTNER)
     hop(1, PARTNER, 3)
     hops(0, 4)
+    for copy in loads[4:]:
+        copy.wait()
+    flush(48)
+    sib_arrived(0)
+    project(0, 0, near)
     hop(2, OWN, 1)
+    project(0, 1, near)
     hop(1, OWN, 4)
     hop(2, PARTNER, 1)
     hop(1, PARTNER, 4)
-    for copy in loads[3:]:
-        copy.wait()
-    sib_arrived(0)
-    project(0, 0, near)
-    project(0, 1, near)
     sib_arrived(1)
     project(1, 0, near)
     project(1, 1, near)
@@ -469,10 +477,10 @@
     project_last(2)
     attend(2)
     give(2)
+    flush(SEQ - 1)
     for j in range(HEADS_HERE):
         take(j)
-    for copy in pending:
-        copy.wait_send()
+    flush(0)
 
 
 def cut(rows, text, image):
@@ -481,7 +489,7 @@
 
 
 def on_device(text_tokens, image_tokens, weights, qk_gain, mod_table, text_lengths, time_index):
-    wraw = jnp.swapaxes(weights, 1, 2)
+    wraw = jnp.transpose(weights, (1, 2, 0, 3))
     cosine, sine = rope_rows()
     vmem = pl.BlockSpec(memory_space=pltpu.VMEM)
     dma = pltpu.SemaphoreType.DMA
@@ -489,9 +497,10 @@
     result = pl.pallas_call(
         kernel,
         out_shape=jax.ShapeDtypeStruct((144, D), BF16),
-        in_specs=[vmem] + [pl.BlockSpec(memory_space=pltpu.HBM)] * 6 + [vmem] * 2,
+        in_specs=[pl.BlockSpec(memory_space=pltpu.HBM)] * 7 + [vmem] * 2,
         out_specs=vmem,
         scratch_shapes=[
+            pltpu.VMEM(wraw.shape, BF16),
             pltpu.VMEM((2, 2, D), F32),
             pltpu.VMEM(text_tokens.shape[1:], BF16),
             pltpu.VMEM(image_tokens.shape[1:], BF16),
@@ -522,7 +531,7 @@
             dma((n_tok,)), dma((n_tok,)),
             dma((3, 7)), dma((3, 7)),
             dma((3,)),
-            dma((6,)),
+            dma((7,)),
         ],
         compiler_params=pltpu.CompilerParams(
             collective_id=0, has_side_effects=True, vmem_limit_bytes=56 * 1024 * 1024

time: 107 us -> 105 us (0.981)
  local copies, waits for them, and re-layouts: 1.93 us -> 0 us
    unnamed x1 -> x0, local copies, waits for them, and re-layouts: 1.93 us -> none
where the time goes in v4:
time: 105 us
  Pallas kernels  103 us (98%)
  between operations  1.93 us (2%)
    pallas_call x1, Pallas kernels, on_device(): pl.pallas_call(kernel, out_shape=jax.ShapeDtypeStruct((144, D), BF16), in...  101 us

profile of v4, /device:TPU:1, one launch (start us, length us, event | category | flops | bytes accessed | tf_op | source)
XLA Modules:
  0.0 105.1 jit_solution(12987601810546201758)
XLA Ops:
  1.9 101.1 %joint_attention.1.rows = bf16[144,3072]{1,0:T(8,128)(2,1)} custom-call(bf16[12,3,2,3072]{3,2,1,0:T(2,128)(2,1)} %bitcast.8, bf16[64,3072]{1,0:T(8,128)(2,1)} %bitcast.10, bf16[72,3072]{1,0:T(8,128)(2,1)} %bitcast.9, f32[28,2,2,3072]{3,2,1,0:T(2,128)} %mods_hbm.1, f32[4,128]{1,0:T(4,128)} %bitcast.11, f32[576,128]{1,0:T(8,128)} %constant.4.clone.cosine_hbm, ...), custom_call_target="tpu_custom_call" | custom-call | flops 9500000256 | bytes 30000000 | tf_op jit(solution)/shard_map/joint_attention/pallas_call | solution.py:497
  103.0 2.1 %cut_outputs.1 = (bf16[1,64,3072]{2,1,0:T(8,128)(2,1)}, bf16[1,72,3072]{2,1,0:T(8,128)(2,1)}) custom-call(bf16[144,3072]{1,0:T(8,128)(2,1)} %joint_attention.1.rows), custom_call_target="tpu_custom_call" | custom-call | tf_op jit(solution)/shard_map/cut_outputs/pallas_call | solution.py:546

commit v5 on v4

--- a/solution.py
+++ b/solution.py
@@ -461,14 +461,14 @@
     hop(2, PARTNER, 3)
     project(1, 0, distant)
     project(1, 1, distant)
+    hop(2, OWN, 4)
+    hop(2, PARTNER, 4)
+    attend(1)
+    give(1)
     cross_arrived(2, (1, 2, 4, 5))
     sib_arrived(2, (0, 1, 2, 4, 5))
     project_some(2, 0, order[0:2])
-    hop(2, OWN, 4)
-    hop(2, PARTNER, 4)
     project_some(2, 1, order[0:2])
-    attend(1)
-    give(1)
     cross_arrived(2, (3, 6, 7))
     sib_arrived(2, (3, 6))
     project_some(2, 0, order[2:3])

time: 105 us -> 106 us (level)
  no operation moved by 1% of the time
where the time goes in v5:
time: 106 us
  Pallas kernels  104 us (98%)
  between operations  1.93 us (2%)
    pallas_call x1, Pallas kernels, on_device(): pl.pallas_call(kernel, out_shape=jax.ShapeDtypeStruct((144, D), BF16), in...  102 us

profile of v5, /device:TPU:1, one launch (start us, length us, event | category | flops | bytes accessed | tf_op | source)
XLA Modules:
  0.0 105.8 jit_solution(815306524195376291)
XLA Ops:
  1.9 101.8 %joint_attention.1.rows = bf16[144,3072]{1,0:T(8,128)(2,1)} custom-call(bf16[12,3,2,3072]{3,2,1,0:T(2,128)(2,1)} %bitcast.8, bf16[64,3072]{1,0:T(8,128)(2,1)} %bitcast.10, bf16[72,3072]{1,0:T(8,128)(2,1)} %bitcast.9, f32[28,2,2,3072]{3,2,1,0:T(2,128)} %mods_hbm.1, f32[4,128]{1,0:T(4,128)} %bitcast.11, f32[576,128]{1,0:T(8,128)} %constant.4.clone.cosine_hbm, ...), custom_call_target="tpu_custom_call" | custom-call | flops 9500000256 | bytes 30000000 | tf_op jit(solution)/shard_map/joint_attention/pallas_call | solution.py:497
  103.7 2.1 %cut_outputs.1 = (bf16[1,64,3072]{2,1,0:T(8,128)(2,1)}, bf16[1,72,3072]{2,1,0:T(8,128)(2,1)}) custom-call(bf16[144,3072]{1,0:T(8,128)(2,1)} %joint_attention.1.rows), custom_call_target="tpu_custom_call" | custom-call | tf_op jit(solution)/shard_map/cut_outputs/pallas_call | solution.py:546
